TPU v7x, 256 devices: a whole 4x4x8 slice. The times are simulated.
256 devices in a mesh: ha: 8 (over z), wa: 32 (over x, y, core).
Axes of the slice: x: 4, y: 4, z: 8, core: 2. Of those that a mesh axis runs over, the one named last changes fastest.
Arguments:
- tokens: bfloat16 [64, 512, 512], P('ha', 'wa'), may hold values from -6 to 6
- cotangent: bfloat16 [64, 512, 512], P('ha', 'wa'), may hold values from -6 to 6
- state_in: float32 [64, 512, 16], P('ha', 'wa'), may hold values from -0.25 to 0.25
- state_out: float32 [64, 512, 16], P('ha', 'wa'), may hold values from -0.25 to 0.25
- width_decay: float32 [64, 512, 8], P('ha', 'wa'), may hold values from -1.6 to 0
- height_decay: float32 [64, 512, 8], P('ha', 'wa'), may hold values from -1.6 to 0
Outputs:
- tokens_grad: float32 [64, 512, 512], P('ha', 'wa')
- state_in_grad: float32 [64, 512, 16], P('ha', 'wa')
- state_out_grad: float32 [64, 512, 16], P('ha', 'wa')
- width_decay_grad: float32 [64, 512, 8], P('ha', 'wa')
- height_decay_grad: float32 [64, 512, 8], P('ha', 'wa')
All inputs are finite; a program needn't handle non-finite values.
Results may differ from a plain program's by a relative error of at most 0.0003.
Values sent between devices are 32-bit elements; how exact they have to be, the bound alone decides.
No kernel may reach another device: no remote copies, remote signals or barrier semaphores. Data moves between devices by JAX's collectives and lax.ppermute only.
A program may use at most 128 MiB of HBM per device.

v0:
```python
import jax
import jax.numpy as jnp
from jax import lax
from jax.experimental import pallas as pl
from jax.experimental.pallas import tpu as pltpu
from jax.sharding import PartitionSpec as P

F32 = jnp.float32
BF16 = jnp.bfloat16

SEG = 8
ROWS = 8
COLS = 16
CH = 64
N = 16
LANES = SEG * N
STEP = 16

X0, C0, B0, S0, D0 = 0, 64, 128, 144, 160
SENT = 168
BACK = 104
EDGE = 40


def spread(ref, at, wide, place):
    for pair in range(ROWS // 2):
        block = ref[:, at + pair * COLS : at + (pair + 1) * COLS, :].reshape(SEG * COLS, 2 * CH)
        flipped = block.T.astype(BF16)
        for two in range(COLS // 2):
            out = jnp.dot(flipped, place[:, two * 256 : (two + 1) * 256], preferred_element_type=F32)
            for part in range(2):
                for half in range(2):
                    wide[2 * two + half, 2 * pair + part] = out[
                        part * CH : (part + 1) * CH, half * LANES : (half + 1) * LANES
                    ]


def make_place(place):
    k = lax.broadcasted_iota(jnp.int32, (LANES, 256), 0)
    m = lax.broadcasted_iota(jnp.int32, (LANES, 256), 1)
    for two in range(COLS // 2):
        col = 2 * two + m // LANES
        hit = k == ((m % LANES) // N) * COLS + col
        place[:, two * 256 : (two + 1) * 256] = jnp.where(hit, 1.0, 0.0).astype(BF16)


def small(ref, bt, ct, wr, hr):
    bt[...] = ref[:, B0 : B0 + N, :].reshape(LANES, 128).T.reshape(COLS, ROWS, LANES)
    ct[...] = ref[:, S0 : S0 + N, :].reshape(LANES, 128).T.reshape(COLS, ROWS, LANES)
    for row, out in ((D0, wr), (D0 + 1, hr)):
        rate = jnp.exp(ref[:, row : row + 1, :])
        wide = jnp.broadcast_to(rate, (SEG, N, 128)).reshape(LANES, 128)
        out[...] = wide.T.reshape(COLS, ROWS, LANES)


def carry_scan(ends, rates, down):
    lane = lax.broadcasted_iota(jnp.int32, (1, LANES), 1)
    keep = (lane >= N) if down else (lane < LANES - N)

    def move(v, by):
        return pltpu.roll(v, by * N if down else LANES - by * N, 1)

    one = jnp.where(keep, move(rates, 1), 0.0)
    two = one * move(one, 1)
    four = two * move(two, 2)

    def run(e):
        f = jnp.where(keep, move(e, 1), 0.0)
        f = f + one * move(f, 1)
        f = f + two * move(f, 2)
        return f + four * move(f, 4)

    return run(ends)


def segment_rate(hr, col):
    rate = hr[col, 0:1, :]
    for row in range(1, ROWS):
        rate = rate * hr[col, row : row + 1, :]
    return jnp.broadcast_to(rate, (ROWS, LANES))


def edges_kernel(ref, edge, back, place, xe, ce, bt, ct, wr, hr, tail, head):
    make_place(place)
    small(ref, bt, ct, wr, hr)
    spread(ref, X0, xe, place)
    spread(ref, C0, ce, place)

    def ends(col, keep):
        rate = segment_rate(hr, col)[0:1]
        for c in range(0, CH, STEP):
            carry = jnp.zeros((STEP, LANES), F32)
            for row in reversed(range(ROWS)):
                carry = hr[col, row : row + 1, :] * (
                    carry + ct[col, row : row + 1, :] * ce[col, row, c : c + STEP, :]
                )
            back[col, c : c + STEP, :] = carry_scan(carry, rate, False)
        return keep

    lax.fori_loop(0, COLS, ends, 0)
    tail[...] = jnp.zeros_like(tail)
    head[...] = jnp.zeros_like(head)

    def sums(step, after):
        col = COLS - 1 - step
        weights = [after[r] * bt[col, r : r + 1, :] for r in range(ROWS)]
        for c in range(0, CH, STEP):
            carry = back[col, c : c + STEP, :]
            for row in reversed(range(ROWS)):
                grad = carry + ct[col, row : row + 1, :] * ce[col, row, c : c + STEP, :]
                carry = hr[col, row : row + 1, :] * grad
                head[row, c : c + STEP, :] = wr[col, row : row + 1, :] * (
                    head[row, c : c + STEP, :] + grad
                )
                tail[row, c : c + STEP, :] += weights[row] * xe[col, row, c : c + STEP, :]
        return tuple(after[r] * wr[col, r : r + 1, :] for r in range(ROWS))

    total = lax.fori_loop(0, COLS, sums, tuple(jnp.ones((1, LANES), F32) for r in range(ROWS)))
    for row in range(ROWS):
        for q in range(CH // STEP):
            at = row * (CH // STEP) + q
            edge[at, 0:STEP, :] = tail[row, q * STEP : (q + 1) * STEP, :]
            edge[at, STEP : 2 * STEP, :] = head[row, q * STEP : (q + 1) * STEP, :]
            edge[at, 2 * STEP :, :] = jnp.broadcast_to(total[row], (EDGE - 2 * STEP, LANES))


def chain_kernel(got, out):
    count = got.shape[0]

    def right(place, carry):
        out[place, 0:STEP, :] = carry
        return got[place, 2 * STEP : 2 * STEP + 1, :] * carry + got[place, 0:STEP, :]

    def left(hop, carry):
        place = count - 1 - hop
        out[place, STEP : 2 * STEP, :] = carry
        return got[place, 2 * STEP : 2 * STEP + 1, :] * carry + got[place, STEP : 2 * STEP, :]

    def both(hop, carry):
        return right(hop, carry[0]), left(hop, carry[1])

    zero = jnp.zeros((STEP, LANES), F32)
    lax.fori_loop(0, count, both, (zero, zero), unroll=4)


def grads_kernel(
    ref, edge, back, out, place, xe, ce, bt, ct, wr, hr, states, front, run, pieces, gather, sums, acc
):
    make_place(place)
    small(ref, bt, ct, wr, hr)
    spread(ref, X0, xe, place)
    spread(ref, C0, ce, place)
    k = lax.broadcasted_iota(jnp.int32, (2 * LANES, 128), 0)
    m = lax.broadcasted_iota(jnp.int32, (2 * LANES, 128), 1)
    for col in range(COLS):
        gather[col] = jnp.where(m == ((k % LANES) // N) * COLS + col, 1.0, 0.0).astype(BF16)
    for row in range(ROWS):
        for q in range(CH // STEP):
            at = row * (CH // STEP) + q
            states[0, row, q * STEP : (q + 1) * STEP, :] = edge[at, 0:STEP, :]
            run[row, q * STEP : (q + 1) * STEP, :] = edge[at, STEP : 2 * STEP, :]

    def forward(col, keep):
        rate = segment_rate(hr, col)[0:1]
        for c in range(0, CH, STEP):
            total = jnp.zeros((STEP, LANES), F32)
            for row in range(ROWS):
                state = (
                    wr[col, row : row + 1, :] * states[col, row, c : c + STEP, :]
                    + bt[col, row : row + 1, :] * xe[col, row, c : c + STEP, :]
                )
                states[col + 1, row, c : c + STEP, :] = state
                total = hr[col, row : row + 1, :] * total + state
            front[col, c : c + STEP, :] = carry_scan(total, rate, True)
        return keep

    lax.fori_loop(0, COLS, forward, 0)

    def fold(v):
        return v[0:8] + v[8:16]

    def products(step, keep):
        col = COLS - 1 - step
        in_sum = [jnp.zeros((8, LANES), F32) for r in range(ROWS)]
        out_sum = [jnp.zeros((8, LANES), F32) for r in range(ROWS)]
        w_sum = [jnp.zeros((8, LANES), F32) for r in range(ROWS)]
        h_sum = [jnp.zeros((8, LANES), F32) for r in range(ROWS)]
        for c in range(0, CH, STEP):
            carry = back[col, c : c + STEP, :]
            grads = [None] * ROWS
            for row in reversed(range(ROWS)):
                grads[row] = carry + ct[col, row : row + 1, :] * ce[col, row, c : c + STEP, :]
                carry = hr[col, row : row + 1, :] * grads[row]
            total = front[col, c : c + STEP, :]
            for row in range(ROWS):
                h_sum[row] = h_sum[row] + fold(grads[row] * total)
                total = hr[col, row : row + 1, :] * total + states[col + 1, row, c : c + STEP, :]
                out_sum[row] = out_sum[row] + fold(total * ce[col, row, c : c + STEP, :])
                grad = grads[row] + run[row, c : c + STEP, :]
                run[row, c : c + STEP, :] = wr[col, row : row + 1, :] * grad
                w_sum[row] = w_sum[row] + fold(grad * states[col, row, c : c + STEP, :])
                in_sum[row] = in_sum[row] + fold(grad * xe[col, row, c : c + STEP, :])
                piece = grad * bt[col, row : row + 1, :]
                high = piece.astype(BF16)
                pieces[col, row * CH + c : row * CH + c + STEP, 0:LANES] = high
                pieces[col, row * CH + c : row * CH + c + STEP, LANES:] = (
                    piece - high.astype(F32)
                ).astype(BF16)
        for row in range(ROWS):
            for which, value in enumerate((in_sum, out_sum, w_sum, h_sum)):
                sums[which, col, row : row + 1, :] = jnp.sum(value[row], axis=0, keepdims=True)
        return keep

    lax.fori_loop(0, COLS, products, 0)
    acc[...] = jnp.zeros_like(acc)

    def collect(col, keep):
        acc[...] += jnp.dot(pieces[col], gather[col], preferred_element_type=F32)
        return keep

    lax.fori_loop(0, COLS, collect, 0)
    for pair in range(ROWS // 2):
        block = acc[pair * 2 * CH : (pair + 1) * 2 * CH, :].T
        out[:, pair * COLS : (pair + 1) * COLS, :] = block.reshape(SEG, COLS, 2 * CH)
    for which in range(2):
        flat = sums[which].reshape(COLS * ROWS, LANES).T
        out[:, 64 + which * N : 64 + (which + 1) * N, :] = flat.reshape(SEG, N, COLS * ROWS)
    for which in range(2):
        flat = sums[2 + which].reshape(COLS * ROWS, LANES).T.reshape(SEG, N, COLS * ROWS)
        rate = jnp.exp(ref[:, D0 + which : D0 + which + 1, :])
        out[:, 96 + which : 97 + which, :] = rate * jnp.sum(flat, axis=1, keepdims=True)
    out[:, 98:, :] = jnp.zeros((SEG, BACK - 98, 128), F32)


WIDE = (COLS, ROWS, CH, LANES)
TOKEN = (COLS, ROWS, LANES)


def vm(shape, kind=F32):
    return pltpu.VMEM(shape, kind)


PARAMS = pltpu.CompilerParams(vmem_limit_bytes=56 * 1024 * 1024)


def per_device(tokens, cotangent, state_in, state_out, width_decay, height_decay):
    def by_group(a):
        a = a.astype(F32).reshape(ROWS // 2, 2, COLS, SEG, CH)
        return jnp.transpose(a, (3, 0, 2, 1, 4)).reshape(SEG, 64, 128)

    def to_all(a):
        flat = jnp.transpose(a, (2, 1, 0)).reshape(1, N, COLS * ROWS)
        return jnp.broadcast_to(flat, (SEG, N, COLS * ROWS))

    def decay(a):
        return jnp.transpose(a, (2, 1, 0)).reshape(SEG, 1, COLS * ROWS)

    message = jnp.concatenate(
        [
            by_group(tokens),
            by_group(cotangent),
            to_all(state_in),
            to_all(state_out),
            decay(width_decay),
            decay(height_decay),
            jnp.zeros((SEG, SENT - 162, 128), F32),
        ],
        axis=1,
    )
    tile = lax.all_to_all(message, "ha", 0, 0, tiled=True)
    devices = lax.axis_size("wa")
    base = [vm((128, 2048), BF16), vm(WIDE), vm(WIDE), vm(TOKEN), vm(TOKEN), vm(TOKEN), vm(TOKEN)]
    edge, back = pl.pallas_call(
        edges_kernel,
        out_shape=(
            jax.ShapeDtypeStruct((devices, EDGE, LANES), F32),
            jax.ShapeDtypeStruct((COLS, CH, LANES), F32),
        ),
        scratch_shapes=base + [vm((ROWS, CH, LANES)), vm((ROWS, CH, LANES))],
        compiler_params=PARAMS,
    )(tile)
    edge = lax.all_to_all(edge, "wa", 0, 0, tiled=True)
    carries = pl.pallas_call(
        chain_kernel,
        out_shape=jax.ShapeDtypeStruct((devices, 2 * STEP, LANES), F32),
        compiler_params=PARAMS,
    )(edge)
    carries = lax.all_to_all(carries, "wa", 0, 0, tiled=True)
    grads = pl.pallas_call(
        grads_kernel,
        out_shape=jax.ShapeDtypeStruct((SEG, BACK, 128), F32),
        scratch_shapes=base
        + [
            vm((COLS + 1,) + WIDE[1:]),
            vm((COLS, CH, LANES)),
            vm((ROWS, CH, LANES)),
            vm((COLS, ROWS * CH, 2 * LANES), BF16),
            vm((COLS, 2 * LANES, 128), BF16),
            vm((4,) + TOKEN),
            vm((ROWS * CH, 128)),
        ],
        compiler_params=PARAMS,
    )(tile, carries, back)
    grads = lax.all_to_all(grads, "ha", 0, 0, tiled=True)
    tokens_grad = grads[:, :64].reshape(SEG, ROWS // 2, COLS, 2, CH)
    tokens_grad = jnp.transpose(tokens_grad, (1, 3, 2, 0, 4)).reshape(ROWS, COLS, SEG * CH)

    def summed(a):
        return jnp.transpose(jnp.sum(a, axis=0).reshape(N, COLS, ROWS), (2, 1, 0))

    def decays(a):
        return jnp.transpose(a.reshape(SEG, COLS, ROWS), (2, 1, 0))

    return (
        tokens_grad,
        summed(grads[:, 64:80]),
        summed(grads[:, 80:96]),
        decays(grads[:, 96]),
        decays(grads[:, 97]),
    )


def solution(mesh):
    spec = P("ha", "wa", None)
    return jax.shard_map(
        per_device, mesh=mesh, in_specs=(spec,) * 6, out_specs=(spec,) * 5, check_vma=False
    )
```

profile of v0, /device:TPU:1, one launch (start us, length us, event | category | flops | bytes accessed | tf_op | source)
XLA Modules:
  0.0 125.7 jit_solution(1590550724567831699)
XLA Ops:
  0.6 0.9 copy.57
  1.5 0.0 copy-start.2
  1.5 0.1 copy.36
  1.6 0.8 copy-done.2
  2.4 0.0 copy-start.3
  2.4 0.1 copy.38
  2.4 0.7 copy-done.3
  3.1 0.0 copy-start.4
  3.1 0.1 copy.39
  3.2 0.0 copy-start
  3.2 0.1 reshape.58
  3.3 0.6 copy-done.4
  3.9 0.1 copy.40
  4.0 0.1 reshape.59
  4.1 0.1 copy-done
  4.1 0.1 reshape.71
  4.3 0.4 copy.55
  4.7 0.0 copy-start.1
  4.7 0.3 reshape.65
  5.0 0.6 copy-done.1
  5.6 0.1 reshape.73
  5.7 0.4 copy.54
  6.1 0.3 reshape.67
  6.5 0.1 concatenate.3
  6.6 28.4 %all_to_all.20.ref = f32[8,168,128]{2,1,0:T(8,128)} all-to-all(f32[8,168,128]{2,1,0:T(8,128)S(1)} %concatenate.3), channel_id=1, replica_groups=mesh['ha'=8,'wa'=32] {'ha'}, dimensions={0} | all-to-all | bytes 1376256 | tf_op jit(solution)/shard_map/all_to_all | solution.py:270
  34.9 9.8 %shard_map.101 = (f32[32,40,128]{2,1,0:T(8,128)}, f32[16,64,128]{2,1,0:T(8,128)}) custom-call(f32[8,168,128]{2,1,0:T(8,128)} %all_to_all.20.ref), custom_call_target="tpu_custom_call" | custom-call | tf_op jit(solution)/shard_map/pallas_call | solution.py:273
  44.8 22.6 %all_to_all.21.got = f32[32,40,128]{2,1,0:T(8,128)} all-to-all(f32[32,40,128]{2,1,0:T(8,128)} %get-tuple-element.7), channel_id=1, replica_groups=mesh['ha'=8,'wa'=32] {'wa'}, dimensions={0} | all-to-all | bytes 1310720 | tf_op jit(solution)/shard_map/all_to_all | solution.py:282
  67.4 2.0 %shard_map.102 = f32[32,32,128]{2,1,0:T(8,128)} custom-call(f32[32,40,128]{2,1,0:T(8,128)} %all_to_all.21.got), custom_call_target="tpu_custom_call" | custom-call | tf_op jit(solution)/shard_map/pallas_call | solution.py:283
  69.4 15.8 %all_to_all.22.edge = f32[32,32,128]{2,1,0:T(8,128)} all-to-all(f32[32,32,128]{2,1,0:T(8,128)} %shard_map.102), channel_id=1, replica_groups=mesh['ha'=8,'wa'=32] {'wa'}, dimensions={0} | all-to-all | bytes 1048576 | tf_op jit(solution)/shard_map/all_to_all | solution.py:288
  85.2 16.7 %shard_map.103 = f32[8,104,128]{2,1,0:T(8,128)} custom-call(f32[8,168,128]{2,1,0:T(8,128)} %all_to_all.20.ref, f32[32,32,128]{2,1,0:T(8,128)} %all_to_all.22.edge, f32[16,64,128]{2,1,0:T(8,128)} %get-tuple-element.8.back), custom_call_target="tpu_custom_call" | custom-call | tf_op jit(solution)/shard_map/pallas_call | solution.py:289
  101.8 19.3 %all_to_all.23 = f32[8,104,128]{2,1,0:T(8,128)S(1)} all-to-all(f32[8,104,128]{2,1,0:T(8,128)} %shard_map.103), channel_id=1, replica_groups=mesh['ha'=8,'wa'=32] {'ha'}, dimensions={0} | all-to-all | bytes 851968 | tf_op jit(solution)/shard_map/all_to_all | solution.py:304
  121.1 0.1 copy.45
  121.2 0.6 copy.47
  121.9 0.1 reshape_squeeze.7
  122.0 0.7 copy.49
  122.7 0.1 copy.44
  122.8 0.6 copy.46
  123.4 0.1 reshape_squeeze.6
  123.5 0.7 copy.48
  124.2 0.3 reshape.60
  124.5 0.3 copy.43
  124.9 0.9 reshape.61
  (7 shorter events, 0.1 us)
Async XLA Ops:
  1.5 0.8 copy-start.2
  2.4 0.8 copy-start.3
  3.1 0.8 copy-start.4
  3.2 0.9 copy-start
  4.7 0.9 copy-start.1
where the time goes:
time: 126 us
  blocking collectives  86.1 us (68%)
  Pallas kernels  28.5 us (23%)
  local copies, waits for them, and re-layouts  10.4 us (8%)
    all_to_all x1, blocking collectives, per_device(): tile = lax.all_to_all(message, 'ha', 0, 0, tiled=True)  28.4 us
    all_to_all x1, blocking collectives, per_device(): edge = lax.all_to_all(edge, 'wa', 0, 0, tiled=True)  22.6 us
    all_to_all x1, blocking collectives, per_device(): grads = lax.all_to_all(grads, 'ha', 0, 0, tiled=True)  19.3 us
    pallas_call x1, Pallas kernels, per_device(): pl.pallas_call(grads_kernel, out_shape=jax.ShapeDtypeStruct((SEG, BACK, 1...  16.7 us
    all_to_all x1, blocking collectives, per_device(): carries = lax.all_to_all(carries, 'wa', 0, 0, tiled=True)  15.8 us
    pallas_call x1, Pallas kernels, per_device(): pl.pallas_call(edges_kernel, out_shape=(jax.ShapeDtypeStruct((devices, ED...  9.82 us
    unnamed x14, local copies, waits for them, and re-layouts  5.39 us

commit v1 on v0

v1 whole, which is shorter than its diff:
```python
import jax
import jax.numpy as jnp
from jax import lax
from jax.experimental import pallas as pl
from jax.experimental.pallas import tpu as pltpu
from jax.sharding import PartitionSpec as P

F32 = jnp.float32
BF16 = jnp.bfloat16

SEG = 8
ROWS = 8
COLS = 16
CH = 64
N = 16
LANES = SEG * N
TOKENS = ROWS * COLS
STEP = 16
QUART = CH // STEP

X0, C0, B0, S0, D0 = 0, 64, 128, 144, 160
SENT = 168
I0, O0, W0 = 64, 80, 96
BACK = 104
EDGE = 40


def pack_kernel(x, y, b, s, w, h, out):
    low = lax.broadcasted_iota(jnp.int32, (COLS, 128), 1) < CH
    for at, a in ((X0, x), (C0, y)):
        for pair in range(ROWS // 2):
            rows = slice(at + pair * COLS, at + (pair + 1) * COLS)
            for two in range(SEG // 2):
                lanes = slice(two * 128, (two + 1) * 128)
                one = a[2 * pair, :, lanes].astype(F32)
                other = a[2 * pair + 1, :, lanes].astype(F32)
                out[2 * two, rows, :] = jnp.where(low, one, pltpu.roll(other, CH, 1))
                out[2 * two + 1, rows, :] = jnp.where(low, pltpu.roll(one, CH, 1), other)
    for at, a in ((B0, b), (S0, s)):
        flat = a[...].reshape(TOKENS, N).T
        for g in range(SEG):
            out[g, at : at + N, :] = flat
    for at, a in ((D0, w), (D0 + 1, h)):
        flat = a[...].reshape(TOKENS, SEG).T
        for g in range(SEG):
            out[g, at : at + 1, :] = flat[g : g + 1]
    out[:, D0 + 2 :, :] = jnp.zeros((SEG, SENT - D0 - 2, 128), F32)


def unpack_kernel(got, x, b, s, w, h):
    low = lax.broadcasted_iota(jnp.int32, (COLS, 128), 1) < CH
    for pair in range(ROWS // 2):
        rows = slice(pair * COLS, (pair + 1) * COLS)
        for two in range(SEG // 2):
            lanes = slice(two * 128, (two + 1) * 128)
            one = got[2 * two, rows, :]
            other = got[2 * two + 1, rows, :]
            x[2 * pair, :, lanes] = jnp.where(low, one, pltpu.roll(other, CH, 1))
            x[2 * pair + 1, :, lanes] = jnp.where(low, pltpu.roll(one, CH, 1), other)
    for at, a in ((I0, b), (O0, s)):
        flat = got[0, at : at + N, :]
        for g in range(1, SEG):
            flat = flat + got[g, at : at + N, :]
        a[...] = flat.T.reshape(ROWS, COLS, N)
    for at, a in ((W0, w), (W0 + 1, h)):
        flat = jnp.concatenate([got[g, at : at + 1, :] for g in range(SEG)], axis=0)
        a[...] = flat.T.reshape(ROWS, COLS, SEG)


def make_place(place):
    k = lax.broadcasted_iota(jnp.int32, (LANES, 256), 0)
    m = lax.broadcasted_iota(jnp.int32, (LANES, 256), 1)
    for two in range(COLS // 2):
        col = 2 * two + m // LANES
        hit = k == ((m % LANES) // N) * COLS + col
        place[:, two * 256 : (two + 1) * 256] = jnp.where(hit, 1.0, 0.0).astype(BF16)


def flipped(ref, at, pair):
    block = ref[:, at + pair * COLS : at + (pair + 1) * COLS, :].reshape(SEG * COLS, 2 * CH)
    return block.T.astype(BF16)


def spread(ref, at, wide, place):
    for pair in range(ROWS // 2):
        block = flipped(ref, at, pair)
        for two in range(COLS // 2):
            out = jnp.dot(block, place[:, two * 256 : (two + 1) * 256], preferred_element_type=F32)
            for part in range(2):
                for half in range(2):
                    wide[2 * two + half, 2 * pair + part] = out[
                        part * CH : (part + 1) * CH, half * LANES : (half + 1) * LANES
                    ]


def by_column(flat, out):
    for col in range(COLS):
        out[col] = flat[pl.ds(col, ROWS, stride=COLS), :]


def small(ref, flat, bt, ct, wr, hr):
    for at, out in ((B0, bt), (S0, ct)):
        flat[...] = ref[:, at : at + N, :].reshape(LANES, TOKENS).T
        by_column(flat, out)
    for at, out in ((D0, wr), (D0 + 1, hr)):
        rate = jnp.exp(ref[:, at : at + 1, :])
        flat[...] = jnp.broadcast_to(rate, (SEG, N, TOKENS)).reshape(LANES, TOKENS).T
        by_column(flat, out)


def mover(down):
    def move(v, by):
        return pltpu.roll(v, by * N if down else LANES - by * N, 1)

    return move


def inside(down):
    lane = lax.broadcasted_iota(jnp.int32, (1, LANES), 1)
    return (lane >= N) if down else (lane < LANES - N)


def carry_rates(flat, rates, down):
    move = mover(down)
    total = flat[0:COLS, :]
    for row in range(1, ROWS):
        total = total * flat[row * COLS : (row + 1) * COLS, :]
    one = jnp.where(inside(down), move(total, 1), 0.0)
    two = one * move(one, 1)
    rates[0] = one
    rates[1] = two
    rates[2] = two * move(two, 2)


def carry_scan(ends, rates, down):
    move = mover(down)
    keep = inside(down)

    def column(col, none):
        f = jnp.where(keep, move(ends[col], 1), 0.0)
        for k, by in enumerate((1, 2, 4)):
            f = f + rates[k, pl.ds(col, 1), :] * move(f, by)
        ends[col] = f
        return none

    lax.fori_loop(0, COLS, column, 0, unroll=4)


def split(v):
    high = v.astype(BF16)
    return high, (v - high.astype(F32)).astype(BF16)


def edges_kernel(ref, edge, back, place, ce, bt, ct, wr, hr, flat, rates, head):
    make_place(place)
    small(ref, flat, bt, ct, wr, hr)
    carry_rates(flat, rates, False)
    spread(ref, C0, ce, place)

    def ends(col, none):
        carry = jnp.zeros((CH, LANES), F32)
        for row in reversed(range(ROWS)):
            one = slice(row, row + 1)
            carry = hr[col, one, :] * (carry + ct[col, one, :] * ce[col, row])
        back[col] = carry
        return none

    lax.fori_loop(0, COLS, ends, 0, unroll=2)
    carry_scan(back, rates, False)

    after = jnp.ones((ROWS, LANES), F32)
    for col in reversed(range(COLS)):
        flat[col * ROWS : (col + 1) * ROWS, :] = after * bt[col]
        after = after * wr[col]
    r = lax.broadcasted_iota(jnp.int32, (LANES, LANES), 0)
    m = lax.broadcasted_iota(jnp.int32, (LANES, LANES), 1)
    own = r // COLS == m // N
    for pair in range(ROWS // 2):
        block = flipped(ref, X0, pair)
        for part in range(2):
            row = 2 * pair + part
            weight = flat[pl.ds(row, COLS, stride=ROWS), :]
            weight = jnp.where(own, jnp.concatenate([weight] * SEG, axis=0), 0.0)
            high, low = split(weight)
            mine = block[part * CH : (part + 1) * CH]
            tail = jnp.dot(mine, high, preferred_element_type=F32) + jnp.dot(
                mine, low, preferred_element_type=F32
            )
            for q in range(QUART):
                edge[row * QUART + q, 0:STEP, :] = tail[q * STEP : (q + 1) * STEP]
                edge[row * QUART + q, 2 * STEP :, :] = jnp.broadcast_to(
                    after[row : row + 1], (EDGE - 2 * STEP, LANES)
                )

    head[...] = jnp.zeros_like(head)

    def sums(step, none):
        col = COLS - 1 - 2 * step
        carry, carry2 = back[col], back[col - 1]
        for row in reversed(range(ROWS)):
            one = slice(row, row + 1)
            grad = carry + ct[col, one, :] * ce[col, row]
            carry = hr[col, one, :] * grad
            grad2 = carry2 + ct[col - 1, one, :] * ce[col - 1, row]
            carry2 = hr[col - 1, one, :] * grad2
            head[row] = wr[col - 1, one, :] * (wr[col, one, :] * (head[row] + grad) + grad2)
        return none

    lax.fori_loop(0, COLS // 2, sums, 0)
    for row in range(ROWS):
        for q in range(QUART):
            edge[row * QUART + q, STEP : 2 * STEP, :] = head[row, q * STEP : (q + 1) * STEP, :]


def chain_kernel(got, out):
    count = got.shape[0]

    def both(hop, carry):
        right, left = carry
        place = count - 1 - hop
        out[hop, 0:STEP, :] = right
        out[place, STEP : 2 * STEP, :] = left
        right = got[hop, 2 * STEP : 2 * STEP + 1, :] * right + got[hop, 0:STEP, :]
        left = got[place, 2 * STEP : 2 * STEP + 1, :] * left + got[place, STEP : 2 * STEP, :]
        return right, left

    zero = jnp.zeros((STEP, LANES), F32)
    lax.fori_loop(0, count, both, (zero, zero), unroll=8)


def total8(v):
    v = v[0 : CH // 2] + v[CH // 2 :]
    v = v[0 : CH // 4] + v[CH // 4 :]
    return v[0:8] + v[8:16]


def grads_kernel(
    ref, edge, back, out, place, xe, ce, bt, ct, wr, hr, flat, rates, states, front, run, kept, pieces, gather, sums
):
    make_place(place)
    small(ref, flat, bt, ct, wr, hr)
    carry_rates(flat, rates, True)
    spread(ref, X0, xe, place)
    spread(ref, C0, ce, place)
    k = lax.broadcasted_iota(jnp.int32, (2 * LANES, 128), 0)
    m = lax.broadcasted_iota(jnp.int32, (2 * LANES, 128), 1)
    for col in range(COLS):
        gather[col * 2 * LANES : (col + 1) * 2 * LANES, :] = jnp.where(
            m == ((k % LANES) // N) * COLS + col, 1.0, 0.0
        ).astype(BF16)
    for row in range(ROWS):
        for q in range(QUART):
            part = slice(q * STEP, (q + 1) * STEP)
            states[0, row, part, :] = edge[row * QUART + q, 0:STEP, :]
            run[row, part, :] = edge[row * QUART + q, STEP : 2 * STEP, :]

    def forward(col, none):
        total = jnp.zeros((CH, LANES), F32)
        for row in range(ROWS):
            one = slice(row, row + 1)
            state = wr[col, one, :] * states[col, row] + bt[col, one, :] * xe[col, row]
            states[col + 1, row] = state
            total = hr[col, one, :] * total + state
        front[col] = total
        return none

    lax.fori_loop(0, COLS, forward, 0)
    carry_scan(front, rates, True)

    def products(step, none):
        col = COLS - 1 - step
        carry = back[col]
        for row in reversed(range(ROWS)):
            one = slice(row, row + 1)
            grad = carry + ct[col, one, :] * ce[col, row]
            carry = hr[col, one, :] * grad
            kept[row] = grad
        total = front[col]
        for row in range(ROWS):
            one = slice(row, row + 1)
            grad = kept[row]
            sums[3, row, col] = total8(grad * total)
            total = hr[col, one, :] * total + states[col + 1, row]
            sums[1, row, col] = total8(total * ce[col, row])
            grad = grad + run[row]
            run[row] = wr[col, one, :] * grad
            sums[2, row, col] = total8(grad * states[col, row])
            sums[0, row, col] = total8(grad * xe[col, row])
            high, low = split(grad * bt[col, one, :])
            pieces[col, row * CH : (row + 1) * CH, 0:LANES] = high
            pieces[col, row * CH : (row + 1) * CH, LANES:] = low
        return none

    lax.fori_loop(0, COLS, products, 0)
    for pair in range(ROWS // 2):
        rows = slice(pair * 2 * CH, (pair + 1) * 2 * CH)
        block = jnp.zeros((2 * CH, 128), F32)
        for col in range(COLS):
            block = block + jnp.dot(
                pieces[col, rows, :], gather[col * 2 * LANES : (col + 1) * 2 * LANES, :], preferred_element_type=F32
            )
        out[:, pair * COLS : (pair + 1) * COLS, :] = block.T.reshape(SEG, COLS, 2 * CH)
    for which, at in enumerate((I0, O0, W0, W0 + 1)):
        rows = sums.at[which].reshape(TOKENS * 8, LANES)
        value = rows[pl.ds(0, TOKENS, stride=8), :]
        for k in range(1, 8):
            value = value + rows[pl.ds(k, TOKENS, stride=8), :]
        value = value.T.reshape(SEG, N, TOKENS)
        if which < 2:
            out[:, at : at + N, :] = value
        else:
            rate = jnp.exp(ref[:, D0 + which - 2 : D0 + which - 1, :])
            out[:, at : at + 1, :] = rate * jnp.sum(value, axis=1, keepdims=True)
    out[:, W0 + 2 :, :] = jnp.zeros((SEG, BACK - W0 - 2, 128), F32)


WIDE = (COLS, ROWS, CH, LANES)
TOKEN = (COLS, ROWS, LANES)


def vm(shape, kind=F32):
    return pltpu.VMEM(shape, kind)


def call(kernel, ins, outs, scratch, mebibytes):
    whole = pl.BlockSpec(memory_space=pltpu.VMEM)
    shapes = tuple(jax.ShapeDtypeStruct(s, F32) for s in outs)
    single = len(outs) == 1
    return pl.pallas_call(
        kernel,
        out_shape=shapes[0] if single else shapes,
        in_specs=[whole] * ins,
        out_specs=whole if single else (whole,) * len(outs),
        scratch_shapes=scratch,
        compiler_params=pltpu.CompilerParams(vmem_limit_bytes=mebibytes * 1024 * 1024),
    )


SMALL = [vm(TOKEN)] * 4 + [vm((TOKENS, LANES)), vm((3, COLS, LANES))]
PLACE = vm((128, 2048), BF16)


def packs():
    return call(pack_kernel, 6, [(SEG, SENT, 128)], [], 8)


def edges(devices):
    outs = [(devices, EDGE, LANES), (COLS, CH, LANES)]
    return call(edges_kernel, 1, outs, [PLACE, vm(WIDE)] + SMALL + [vm((ROWS, CH, LANES))], 16)


def chains(devices):
    return call(chain_kernel, 1, [(devices, 2 * STEP, LANES)], [], 8)


def grads():
    block = (ROWS, CH, LANES)
    scratch = [PLACE, vm(WIDE), vm(WIDE)] + SMALL
    scratch += [vm((COLS + 1,) + block), vm((COLS, CH, LANES)), vm(block), vm(block)]
    scratch += [
        vm((COLS, ROWS * CH, 2 * LANES), BF16),
        vm((COLS * 2 * LANES, 128), BF16),
        vm((4, ROWS, COLS, 8, LANES)),
    ]
    return call(grads_kernel, 3, [(SEG, BACK, 128)], scratch, 32)


def unpacks():
    outs = [(ROWS, COLS, SEG * CH)] + [(ROWS, COLS, N)] * 2 + [(ROWS, COLS, SEG)] * 2
    return call(unpack_kernel, 1, outs, [], 8)


def per_device(*arrays):
    devices = lax.axis_size("wa")
    tile = lax.all_to_all(packs()(*arrays), "ha", 0, 0, tiled=True)
    edge, back = edges(devices)(tile)
    edge = lax.all_to_all(edge, "wa", 0, 0, tiled=True)
    carries = lax.all_to_all(chains(devices)(edge), "wa", 0, 0, tiled=True)
    answer = grads()(tile, carries, back)
    return unpacks()(lax.all_to_all(answer, "ha", 0, 0, tiled=True))


def solution(mesh):
    spec = P("ha", "wa", None)
    return jax.shard_map(
        per_device, mesh=mesh, in_specs=(spec,) * 6, out_specs=(spec,) * 5, check_vma=False
    )
```

time: 126 us -> 103 us (0.82)
  Pallas kernels: 28.5 us -> 13.1 us
  local copies, waits for them, and re-layouts: 10.4 us -> 4.87 us
  blocking collectives: 86.1 us -> 84 us
    pallas_call x3 -> x5, Pallas kernels: 28.5 us -> 13.1 us  [the longest x1 8.29 us: per_device(): answer = grads()(tile, carries, back)]
    reshape x10 -> x0, local copies, waits for them, and re-layouts: 3.06 us -> none  [the longest x6 1.68 us: by_group(): return jnp.transpose(a, (3, 0, 2, 1, 4)).reshape(SEG, 64, 128)]
    unnamed x14 -> x10, local copies, waits for them, and re-layouts: 5.39 us -> 3.48 us
    all_to_all x3, blocking collectives: 63.5 us -> 61.7 us  [the longest x1 28.3 us: per_device(): tile = lax.all_to_all(packs()(*arrays), 'ha', 0, 0, tiled=True)]
    pallas_call x0 -> x2, local copies, waits for them, and re-layouts: none -> 1.39 us  [per_device(): return unpacks()(lax.all_to_all(answer, 'ha', 0, 0, tiled=True))]
    transpose x5 -> x0, local copies, waits for them, and re-layouts: 1.36 us -> none  [the longest x2 0.89 us: to_all(): flat = jnp.transpose(a, (2, 1, 0)).reshape(1, N, COLS * ROWS)]
where the time goes in v1:
time: 103 us
  blocking collectives  84 us (82%)
  Pallas kernels  13.1 us (13%)
  local copies, waits for them, and re-layouts  4.87 us (5%)
    all_to_all x1, blocking collectives, per_device(): tile = lax.all_to_all(packs()(*arrays), 'ha', 0, 0, tiled=True)  28.3 us
    all_to_all x1, blocking collectives, per_device(): edge = lax.all_to_all(edge, 'wa', 0, 0, tiled=True)  22.3 us
    all_to_all x1, blocking collectives, per_device(): return unpacks()(lax.all_to_all(answer, 'ha', 0, 0, tiled=True))  18.3 us
    all_to_all x1, blocking collectives, per_device(): carries = lax.all_to_all(chains(devices)(edge), 'wa', 0, 0, tiled=True)  15.1 us
    pallas_call x1, Pallas kernels, per_device(): answer = grads()(tile, carries, back)  8.29 us
    pallas_call x1, Pallas kernels, per_device(): edge, back = edges(devices)(tile)  3.71 us
    unnamed x10, local copies, waits for them, and re-layouts  3.48 us

profile of v1, /device:TPU:1, one launch (start us, length us, event | category | flops | bytes accessed | tf_op | source)
XLA Modules:
  0.0 102.7 jit_solution(559083467023076612)
XLA Ops:
  0.6 0.0 copy-start
  0.6 0.9 copy.11.w
  1.5 0.0 copy-start.2
  1.5 0.9 copy.12.h
  2.4 0.0 copy-done
  2.4 0.0 copy-done.2
  2.4 0.0 copy-start.1
  2.4 0.9 copy-done.1
  3.3 0.0 copy-start.3
  3.3 0.8 copy-done.3
  4.2 0.2 shard_map.101
  4.3 28.3 %all_to_all.20.ref = f32[8,168,128]{2,1,0:T(8,128)S(1)} all-to-all(f32[8,168,128]{2,1,0:T(8,128)S(1)} %shard_map.101), channel_id=1, replica_groups=mesh['ha'=8,'wa'=32] {'ha'}, dimensions={0} | all-to-all | bytes 1376256 | tf_op jit(solution)/shard_map/all_to_all | solution.py:375
  32.6 3.7 %shard_map.102 = (f32[32,40,128]{2,1,0:T(8,128)S(1)}, f32[16,64,128]{2,1,0:T(8,128)S(1)}) custom-call(f32[8,168,128]{2,1,0:T(8,128)S(1)} %all_to_all.20.ref), custom_call_target="tpu_custom_call" | custom-call | tf_op jit(solution)/shard_map/pallas_call | solution.py:376
  36.3 22.3 %all_to_all.21.got = f32[32,40,128]{2,1,0:T(8,128)S(1)} all-to-all(f32[32,40,128]{2,1,0:T(8,128)S(1)} %get-tuple-element.7), channel_id=1, replica_groups=mesh['ha'=8,'wa'=32] {'wa'}, dimensions={0} | all-to-all | bytes 1310720 | tf_op jit(solution)/shard_map/all_to_all | solution.py:377
  58.6 0.1 shard_map.103
  58.7 15.1 %all_to_all.22.edge = f32[32,32,128]{2,1,0:T(8,128)S(1)} all-to-all(f32[32,32,128]{2,1,0:T(8,128)S(1)} %shard_map.103), channel_id=1, replica_groups=mesh['ha'=8,'wa'=32] {'wa'}, dimensions={0} | all-to-all | bytes 1048576 | tf_op jit(solution)/shard_map/all_to_all | solution.py:378
  73.9 8.3 %shard_map.104 = f32[8,104,128]{2,1,0:T(8,128)S(1)} custom-call(f32[8,168,128]{2,1,0:T(8,128)S(1)} %all_to_all.20.ref, f32[32,32,128]{2,1,0:T(8,128)S(1)} %all_to_all.22.edge, f32[16,64,128]{2,1,0:T(8,128)S(1)} %get-tuple-element.8.back), custom_call_target="tpu_custom_call" | custom-call | tf_op jit(solution)/shard_map/pallas_call | solution.py:379
  82.2 18.3 %all_to_all.23.got = f32[8,104,128]{2,1,0:T(8,128)S(1)} all-to-all(f32[8,104,128]{2,1,0:T(8,128)S(1)} %shard_map.104), channel_id=1, replica_groups=mesh['ha'=8,'wa'=32] {'ha'}, dimensions={0} | all-to-all | bytes 851968 | tf_op jit(solution)/shard_map/all_to_all | solution.py:380
  100.5 0.9 shard_map.105
  101.3 0.7 copy.13
  102.0 0.7 copy.14
Async XLA Ops:
  0.6 1.8 %copy-start = (bf16[8,16,512]{2,1,0:T(8,128)(2,1)S(1)}, bf16[8,16,512]{2,1,0:T(8,128)(2,1)}, u32[]{:S(2)}) copy-start(bf16[8,16,512]{2,1,0:T(8,128)(2,1)} %x.1) | copy-start | bytes 393220
  1.5 0.9 copy-start.2
  2.4 0.9 copy-start.1
  3.3 0.8 copy-start.3

commit v2 on v1

v2 whole, which is shorter than its diff:
```python
import jax
import jax.numpy as jnp
from jax import lax
from jax.experimental import pallas as pl
from jax.experimental.pallas import tpu as pltpu
from jax.sharding import PartitionSpec as P

F32 = jnp.float32
BF16 = jnp.bfloat16

SEG = 8
ROWS = 8
COLS = 16
CH = 64
N = 16
LANES = SEG * N
TOKENS = ROWS * COLS
STEP = 16
QUART = CH // STEP

X0, C0, B0, S0, D0 = 0, 64, 128, 144, 160
SENT = 168
I0, O0, W0 = 64, 80, 96
BACK = 104
EDGE = 40
UE, US, UF, UP = 2, 1, 1, 1
PK = 60


def make_place(place):
    k = lax.broadcasted_iota(jnp.int32, (LANES, 256), 0)
    m = lax.broadcasted_iota(jnp.int32, (LANES, 256), 1)
    for two in range(COLS // 2):
        col = 2 * two + m // LANES
        hit = k == ((m % LANES) // N) * COLS + col
        place[two] = jnp.where(hit, 1.0, 0.0).astype(BF16)


def make_gather(gather):
    k = lax.broadcasted_iota(jnp.int32, (2 * LANES, 128), 0)
    m = lax.broadcasted_iota(jnp.int32, (2 * LANES, 128), 1)
    for col in range(COLS):
        hit = m == ((k % LANES) // N) * COLS + col
        gather[col] = jnp.where(hit, 1.0, 0.0).astype(BF16)


def pack_kernel(x0, y0, b0, s0, w0, h0, out, x, y, b, s, w, h, done):
    copies = [
        pltpu.make_async_copy(source, target, done.at[k])
        for k, (source, target) in enumerate(((w0, w), (h0, h), (b0, b), (s0, s), (x0, x), (y0, y)))
    ]
    for copy in copies:
        copy.start()
    low = lax.broadcasted_iota(jnp.int32, (COLS, 128), 1) < CH
    out[:, D0 + 2 :, :] = jnp.zeros((SEG, SENT - D0 - 2, 128), F32)
    for k, (at, a) in enumerate(((D0, w), (D0 + 1, h))):
        copies[k].wait()
        flat = jnp.concatenate([a[row] for row in range(ROWS)], axis=1)
        for g in range(SEG):
            out[g, at : at + 1, :] = flat[g : g + 1]
    for k, (at, a) in enumerate(((B0, b), (S0, s))):
        copies[2 + k].wait()
        flat = a[...].reshape(TOKENS, N).T
        for g in range(SEG):
            out[g, at : at + N, :] = flat
    for k, (at, a) in enumerate(((X0, x), (C0, y))):
        copies[4 + k].wait()
        for pair in range(ROWS // 2):
            rows = slice(at + pair * COLS, at + (pair + 1) * COLS)
            for two in range(SEG // 2):
                lanes = slice(two * 128, (two + 1) * 128)
                one = a[2 * pair, :, lanes].astype(F32)
                other = a[2 * pair + 1, :, lanes].astype(F32)
                out[2 * two, rows, :] = jnp.where(low, one, pltpu.roll(other, CH, 1))
                out[2 * two + 1, rows, :] = jnp.where(low, pltpu.roll(one, CH, 1), other)


def unpack_kernel(got, x, b, s, w, h):
    low = lax.broadcasted_iota(jnp.int32, (COLS, 128), 1) < CH
    for pair in range(ROWS // 2):
        rows = slice(pair * COLS, (pair + 1) * COLS)
        for two in range(SEG // 2):
            lanes = slice(two * 128, (two + 1) * 128)
            one = got[2 * two, rows, :]
            other = got[2 * two + 1, rows, :]
            x[2 * pair, :, lanes] = jnp.where(low, one, pltpu.roll(other, CH, 1))
            x[2 * pair + 1, :, lanes] = jnp.where(low, pltpu.roll(one, CH, 1), other)
    for at, a in ((I0, b), (O0, s)):
        flat = got[0, at : at + N, :]
        for g in range(1, SEG):
            flat = flat + got[g, at : at + N, :]
        a[...] = flat.T.reshape(ROWS, COLS, N)
    for at, a in ((W0, w), (W0 + 1, h)):
        flat = jnp.concatenate([got[g, at : at + 1, :] for g in range(SEG)], axis=0)
        for row in range(ROWS):
            a[row] = flat[:, row * COLS : (row + 1) * COLS]


def flip(ref, at, flipped):
    for pair in range(ROWS // 2):
        block = ref[:, at + pair * COLS : at + (pair + 1) * COLS, :].reshape(SEG * COLS, 2 * CH)
        flipped[pair * 2 * CH : (pair + 1) * 2 * CH, :] = block.T.astype(BF16)


def spread(flipped, place, wide, two):
    for pair in range(ROWS // 2):
        block = flipped[pair * 2 * CH : (pair + 1) * 2 * CH, :]
        out = jnp.dot(block, place[two], preferred_element_type=F32)
        for part in range(2):
            for half in range(2):
                wide[2 * two + half, 2 * pair + part] = out[
                    part * CH : (part + 1) * CH, half * LANES : (half + 1) * LANES
                ]


def by_column(flat, out):
    for col in range(COLS):
        out[col] = flat[pl.ds(col, ROWS, stride=COLS), :]


def small(ref, flat, bt, ct, wr, hr):
    for at, out in ((B0, bt), (S0, ct)):
        flat[...] = ref[:, at : at + N, :].reshape(LANES, TOKENS).T
        by_column(flat, out)
    for at, out in ((D0, wr), (D0 + 1, hr)):
        rate = jnp.exp(ref[:, at : at + 1, :])
        flat[...] = jnp.broadcast_to(rate, (SEG, N, TOKENS)).reshape(LANES, TOKENS).T
        by_column(flat, out)


def tables(rows):
    return [rows.at[:, k * ROWS : (k + 1) * ROWS, :] for k in range(5)]


def mover(down):
    def move(v, by):
        return pltpu.roll(v, by * N if down else LANES - by * N, 1)

    return move


def inside(down):
    lane = lax.broadcasted_iota(jnp.int32, (1, LANES), 1)
    return (lane >= N) if down else (lane < LANES - N)


def carry_rates(flat, rates, down):
    move = mover(down)
    total = flat[0:COLS, :]
    for row in range(1, ROWS):
        total = total * flat[row * COLS : (row + 1) * COLS, :]
    one = jnp.where(inside(down), move(total, 1), 0.0)
    two = one * move(one, 1)
    rates[:, 0, :] = one
    rates[:, 1, :] = two
    rates[:, 2, :] = two * move(two, 2)


def carry_scan(ends, rates, down):
    move = mover(down)
    keep = inside(down)

    def column(col, none):
        f = jnp.where(keep, move(ends[col], 1), 0.0)
        for k, by in enumerate((1, 2, 4)):
            f = f + rates[col, k : k + 1, :] * move(f, by)
        ends[col] = f
        return none

    lax.fori_loop(0, COLS, column, 0, unroll=4)


def split(v):
    high = v.astype(BF16)
    return high, (v - high.astype(F32)).astype(BF16)


def own_segment():
    r = lax.broadcasted_iota(jnp.int32, (LANES, LANES), 0)
    m = lax.broadcasted_iota(jnp.int32, (LANES, LANES), 1)
    return r // COLS == m // N


def diagonal(flat, row, own):
    value = flat[pl.ds(row, COLS, stride=ROWS), :]
    return jnp.where(own, jnp.concatenate([value] * SEG, axis=0), 0.0)


def edges_kernel(ref, edge, back, rows, place, ce, flat, rates, head, flipped):
    make_place(place)
    bt, ct, wr, hr, down = tables(rows)
    small(ref, flat, bt, ct, wr, hr)
    carry_rates(flat, rates, False)
    carry_rates(flat, down, True)
    flip(ref, C0, flipped)
    for two in range(COLS // 2):
        spread(flipped, place, ce, two)

    def ends(col, none):
        carry = jnp.zeros((CH, LANES), F32)
        for row in reversed(range(ROWS)):
            one = slice(row, row + 1)
            carry = hr[col, one, :] * (carry + ct[col, one, :] * ce[col, row])
        back[col] = carry
        return none

    lax.fori_loop(0, COLS, ends, 0, unroll=UE)
    carry_scan(back, rates, False)

    after = jnp.ones((ROWS, LANES), F32)
    for col in reversed(range(COLS)):
        flat[col * ROWS : (col + 1) * ROWS, :] = after * bt[col]
        after = after * wr[col]
    own = own_segment()
    flip(ref, X0, flipped)
    for pair in range(ROWS // 2):
        for part in range(2):
            row = 2 * pair + part
            high, low = split(diagonal(flat, row, own))
            mine = flipped[row * CH : (row + 1) * CH, :]
            tail = jnp.dot(mine, high, preferred_element_type=F32) + jnp.dot(
                mine, low, preferred_element_type=F32
            )
            for q in range(QUART):
                edge[row * QUART + q, 0:STEP, :] = tail[q * STEP : (q + 1) * STEP]
                edge[row * QUART + q, 2 * STEP :, :] = jnp.broadcast_to(
                    after[row : row + 1], (EDGE - 2 * STEP, LANES)
                )

    head[...] = jnp.zeros_like(head)

    def sums(step, none):
        col = COLS - 1 - 2 * step
        carry, carry2 = back[col], back[col - 1]
        for row in reversed(range(ROWS)):
            one = slice(row, row + 1)
            grad = carry + ct[col, one, :] * ce[col, row]
            carry = hr[col, one, :] * grad
            grad2 = carry2 + ct[col - 1, one, :] * ce[col - 1, row]
            carry2 = hr[col - 1, one, :] * grad2
            head[row] = wr[col - 1, one, :] * (wr[col, one, :] * (head[row] + grad) + grad2)
        return none

    lax.fori_loop(0, COLS // 2, sums, 0, unroll=US)
    for row in range(ROWS):
        for q in range(QUART):
            edge[row * QUART + q, STEP : 2 * STEP, :] = head[row, q * STEP : (q + 1) * STEP, :]


def chain_kernel(got, out):
    count = got.shape[0]

    def both(hop, carry):
        right, left = carry
        place = count - 1 - hop
        out[hop, 0:STEP, :] = right
        out[place, STEP : 2 * STEP, :] = left
        right = got[hop, 2 * STEP : 2 * STEP + 1, :] * right + got[hop, 0:STEP, :]
        left = got[place, 2 * STEP : 2 * STEP + 1, :] * left + got[place, STEP : 2 * STEP, :]
        return right, left

    zero = jnp.zeros((STEP, LANES), F32)
    lax.fori_loop(0, count, both, (zero, zero), unroll=8)


def total8(v):
    v = v[0 : CH // 2] + v[CH // 2 :]
    v = v[0 : CH // 4] + v[CH // 4 :]
    return v[0:8] + v[8:16]


def local_kernel(
    ref, back, place, table, out, high, low,
    gather, xe, ce, states, front, run, kept, pieces, sums, flipped, flat
):
    bt, ct, wr, hr, rates = tables(table)
    make_gather(gather)
    value = jnp.ones((ROWS, LANES), F32)
    for col in reversed(range(COLS)):
        flat[col * ROWS : (col + 1) * ROWS, :] = value * bt[col]
        value = value * wr[col]
    own = own_segment()
    for row in range(ROWS):
        high[row], low[row] = split(diagonal(flat, row, own))
    flip(ref, X0, flipped)
    for two in range(COLS // 2):
        spread(flipped, place, xe, two)
    flip(ref, C0, flipped)
    for two in range(COLS // 2):
        spread(flipped, place, ce, two)
    states[0] = jnp.zeros(BLOCK, F32)
    run[...] = jnp.zeros(BLOCK, F32)

    def forward(col, none):
        total = jnp.zeros((CH, LANES), F32)
        for row in range(ROWS):
            one = slice(row, row + 1)
            state = wr[col, one, :] * states[col, row] + bt[col, one, :] * xe[col, row]
            states[col + 1, row] = state
            total = hr[col, one, :] * total + state
        front[col] = total
        return none

    lax.fori_loop(0, COLS, forward, 0, unroll=UF)
    carry_scan(front, rates, True)

    def products(step, none):
        col = COLS - 1 - step
        carry = back[col]
        for row in reversed(range(ROWS)):
            one = slice(row, row + 1)
            grad = carry + ct[col, one, :] * ce[col, row]
            carry = hr[col, one, :] * grad
            kept[row] = grad
        total = front[col]
        for row in range(ROWS):
            one = slice(row, row + 1)
            grad = kept[row]
            sums[3, row, col] = total8(grad * total)
            total = hr[col, one, :] * total + states[col + 1, row]
            sums[1, row, col] = total8(total * ce[col, row])
            grad = grad + run[row]
            run[row] = wr[col, one, :] * grad
            sums[2, row, col] = total8(grad * states[col, row])
            sums[0, row, col] = total8(grad * xe[col, row])
            high, low = split(grad * bt[col, one, :])
            pieces[col, row * CH : (row + 1) * CH, 0:LANES] = high
            pieces[col, row * CH : (row + 1) * CH, LANES:] = low
        return none

    lax.fori_loop(0, COLS, products, 0, unroll=UP)
    for pair in range(ROWS // 2):
        rows = slice(pair * 2 * CH, (pair + 1) * 2 * CH)
        block = jnp.zeros((2 * CH, 128), F32)
        for col in range(COLS):
            block = block + jnp.dot(pieces[col, rows, :], gather[col], preferred_element_type=F32)
        out[:, pair * COLS : (pair + 1) * COLS, :] = block.T.reshape(SEG, COLS, 2 * CH)
    for which, at in enumerate((I0, O0, W0, W0 + 1)):
        put(ref, out, at, over_sublanes(sums.at[which]))
    out[:, W0 + 2 :, :] = jnp.zeros((SEG, BACK - W0 - 2, 128), F32)


def over_sublanes(part):
    rows = part.reshape(TOKENS * 8, LANES)
    value = rows[pl.ds(0, TOKENS, stride=8), :]
    for k in range(1, 8):
        value = value + rows[pl.ds(k, TOKENS, stride=8), :]
    return value


def put(ref, out, at, value, old=None):
    value = value.T.reshape(SEG, N, TOKENS)
    size = N
    if at >= W0:
        rate = jnp.exp(ref[:, D0 + at - W0 : D0 + at - W0 + 1, :])
        value, size = rate * jnp.sum(value, axis=1, keepdims=True), 1
    if old is not None:
        value = value + old[:, at : at + size, :]
    out[:, at : at + size, :] = value


def outer_kernel(
    ref, edge, local, back, place, table, high, low, out,
    before, after, ce, front, kept, sums, flipped, left, right, flat, raw, meet
):
    bt, ct, wr, hr, rates = tables(table)
    value = jnp.ones((ROWS, LANES), F32)
    for col in range(COLS):
        value = value * wr[col]
        before[col] = value
    value = jnp.ones((ROWS, LANES), F32)
    for col in reversed(range(COLS)):
        after[col] = value
        value = value * wr[col]
    flip(ref, C0, flipped)
    for two in range(COLS // 2):
        spread(flipped, place, ce, two)
    for row in range(ROWS):
        for q in range(QUART):
            part = slice(q * STEP, (q + 1) * STEP)
            left[row, part, :] = edge[row * QUART + q, 0:STEP, :]
            right[row, part, :] = edge[row * QUART + q, STEP : 2 * STEP, :]

    def forward(col, none):
        total = jnp.zeros((CH, LANES), F32)
        for row in range(ROWS):
            one = slice(row, row + 1)
            total = hr[col, one, :] * total + before[col, one, :] * left[row]
        front[col] = total
        return none

    lax.fori_loop(0, COLS, forward, 0)
    carry_scan(front, rates, True)

    def products(col, none):
        carry = back[col]
        for row in reversed(range(ROWS)):
            one = slice(row, row + 1)
            grad = carry + ct[col, one, :] * ce[col, row]
            carry = hr[col, one, :] * grad
            kept[row] = grad
            sums[2, row, col] = total8(grad * left[row])
        total = front[col]
        for row in range(ROWS):
            one = slice(row, row + 1)
            sums[1, row, col] = total8(kept[row] * total)
            total = hr[col, one, :] * total + before[col, one, :] * left[row]
            sums[0, row, col] = total8(total * ce[col, row])
        return none

    lax.fori_loop(0, COLS, products, 0)

    own = own_segment()
    none = jnp.zeros((CH, LANES), BF16)
    half = lax.broadcasted_iota(jnp.int32, (LANES, 128), 1) < CH
    for pair in range(ROWS // 2):
        rows = slice(pair * COLS, (pair + 1) * COLS)
        tokens = ref[:, rows, :].reshape(SEG * COLS, 2 * CH).astype(BF16)
        parts = [split(right[2 * pair + part]) for part in range(2)]
        both = [jnp.concatenate([parts[0][k], parts[1][k]], axis=0) for k in range(2)]
        found = []
        for part in range(2):
            row = 2 * pair + part
            value = jnp.zeros((LANES, LANES), F32)
            for k in range(2):
                pieces = [parts[0][k], none] if part == 0 else [none, parts[1][k]]
                value = value + jnp.dot(tokens, jnp.concatenate(pieces, axis=0), preferred_element_type=F32)
            value = jnp.where(own, value, 0.0).reshape(SEG, COLS, LANES)
            raw[row * COLS : (row + 1) * COLS, :] = jnp.sum(value, axis=0)
            meet[row : row + 1, :] = jnp.sum(right[row] * left[row], axis=0, keepdims=True)
            value = jnp.zeros((LANES, 128), F32)
            for weight, k in ((low, 0), (high, 1), (high, 0)):
                value = value + lax.dot_general(
                    weight[row], both[k], (((1,), (1,)), ((), ())), preferred_element_type=F32
                )
            found.append(value)
        value = jnp.where(half, found[0], found[1]).reshape(SEG, COLS, 128)
        out[:, rows, :] = local[:, rows, :] + value

    put(ref, out, O0, over_sublanes(sums.at[0]), local)
    put(ref, out, W0 + 1, over_sublanes(sums.at[1]), local)
    flat[...] = over_sublanes(sums.at[2])

    def rows_of(a, col):
        return a[pl.ds(col, ROWS, stride=COLS), :]

    value = jnp.zeros((ROWS, LANES), F32)
    terms = [None] * COLS
    for col in reversed(range(COLS)):
        value = rows_of(flat, col) + value
        terms[col] = value * before[col - 1] if col else value
        value = wr[col] * value
    value = meet[...]
    for col in range(COLS):
        terms[col] = terms[col] + after[col] * value
        product = rows_of(raw, col)
        value = wr[col] * value + bt[col] * product
        raw[pl.ds(col, ROWS, stride=COLS), :] = after[col] * product
    for col in range(COLS):
        flat[pl.ds(col, ROWS, stride=COLS), :] = terms[col]
    put(ref, out, I0, raw[...], local)
    put(ref, out, W0, flat[...], local)
    out[:, W0 + 2 :, :] = local[:, W0 + 2 :, :]


WIDE = (COLS, ROWS, CH, LANES)
TOKEN = (COLS, ROWS, LANES)
ENDS = (COLS, CH, LANES)
BLOCK = (ROWS, CH, LANES)
RATES = (COLS, ROWS, LANES)
TABLE = (COLS, 5 * ROWS, LANES)
PLACE = (COLS // 2, LANES, 256)
FLIP = (ROWS * CH, 128)


def vm(shape, kind=F32):
    return pltpu.VMEM(shape, kind)


def call(kernel, ins, outs, scratch, mebibytes, kinds=None, place=pltpu.VMEM, flops=10**8):
    whole = pl.BlockSpec(memory_space=pltpu.VMEM)
    kinds = kinds or (F32,) * len(outs)
    shapes = tuple(jax.ShapeDtypeStruct(s, k) for s, k in zip(outs, kinds))
    single = len(outs) == 1
    return pl.pallas_call(
        kernel,
        out_shape=shapes[0] if single else shapes,
        in_specs=[pl.BlockSpec(memory_space=place)] * ins,
        out_specs=whole if single else (whole,) * len(outs),
        scratch_shapes=scratch,
        compiler_params=pltpu.CompilerParams(vmem_limit_bytes=int(mebibytes * 1024 * 1024)),
        cost_estimate=pl.CostEstimate(flops=flops, bytes_accessed=10**6, transcendentals=0),
    )


def packs():
    scratch = [vm((ROWS, COLS, SEG * CH), BF16)] * 2 + [vm((ROWS, COLS, N))] * 2
    scratch += [vm((ROWS, SEG, COLS))] * 2 + [pltpu.SemaphoreType.DMA((6,))]
    return call(pack_kernel, 6, [(SEG, SENT, 128)], scratch, PK, place=pltpu.HBM)


def edges(devices):
    outs = [(devices, EDGE, LANES), ENDS, TABLE, PLACE]
    scratch = [vm(WIDE), vm((TOKENS, LANES)), vm(RATES), vm(BLOCK), vm(FLIP, BF16)]
    return call(edges_kernel, 1, outs, scratch, 14, kinds=(F32, F32, F32, BF16))


def chains(devices):
    return call(chain_kernel, 1, [(devices, 2 * STEP, LANES)], [], 8)


def local_grads():
    outs = [(SEG, BACK, 128), (ROWS, LANES, LANES), (ROWS, LANES, LANES)]
    scratch = [vm((COLS, 2 * LANES, 128), BF16), vm(WIDE), vm(WIDE), vm((COLS + 1,) + BLOCK), vm(ENDS)]
    scratch += [vm(BLOCK), vm(BLOCK), vm((COLS, ROWS * CH, 2 * LANES), BF16), vm((4, ROWS, COLS, 8, LANES))]
    scratch += [vm(FLIP, BF16), vm((TOKENS, LANES))]
    return call(local_kernel, 4, outs, scratch, 28, kinds=(F32, BF16, BF16), flops=5 * 10**9)


def outer_grads():
    scratch = [vm(TOKEN), vm(TOKEN), vm(WIDE), vm(ENDS), vm(BLOCK), vm((3, ROWS, COLS, 8, LANES))]
    scratch += [vm(FLIP, BF16), vm(BLOCK), vm(BLOCK), vm((TOKENS, LANES)), vm((TOKENS, LANES)), vm((ROWS, LANES))]
    return call(outer_kernel, 8, [(SEG, BACK, 128)], scratch, 16)


def unpacks():
    outs = [(ROWS, COLS, SEG * CH)] + [(ROWS, COLS, N)] * 2 + [(ROWS, SEG, COLS)] * 2
    return call(unpack_kernel, 1, outs, [], 8)


def swapped(a):
    return jnp.transpose(a, (0, 2, 1))


def per_device(tokens, cotangent, state_in, state_out, width_decay, height_decay):
    devices = lax.axis_size("wa")
    message = packs()(
        tokens, cotangent, state_in, state_out, swapped(width_decay), swapped(height_decay)
    )
    tile = lax.all_to_all(message, "ha", 0, 0, tiled=True)
    edge, back, table, place = edges(devices)(tile)
    edge = lax.all_to_all(edge, "wa", 0, 0, tiled=True)
    local, high, low = local_grads()(tile, back, place, table)
    carries = lax.all_to_all(chains(devices)(edge), "wa", 0, 0, tiled=True)
    answer = outer_grads()(tile, carries, local, back, place, table, high, low)
    x, b, s, w, h = unpacks()(lax.all_to_all(answer, "ha", 0, 0, tiled=True))
    return x, b, s, swapped(w), swapped(h)


def solution(mesh):
    spec = P("ha", "wa", None)
    return jax.shard_map(
        per_device, mesh=mesh, in_specs=(spec,) * 6, out_specs=(spec,) * 5, check_vma=False
    )
```

time: 103 us -> 98.6 us (0.957)
  blocking collectives: 84 us -> 69.1 us
  Pallas kernels: 13.1 us -> 21.5 us
  local copies, waits for them, and re-layouts: 4.87 us -> 0 us
  starting transfers between devices: 0 us -> 3.71 us
  waiting for transfers between devices: 0 us -> 3.33 us
    all_to_all x3 -> x2, blocking collectives: 61.7 us -> 46.8 us  [the longest x1 28.5 us: per_device(): tile = lax.all_to_all(message, 'ha', 0, 0, tiled=True)]
    pallas_call x4 -> x5, Pallas kernels: 13.1 us -> 20.6 us  [the longest x1 8.29 us: per_device(): local, high, low = local_grads()(tile, back, place, table)]
    all_to_all x0 -> x1, starting transfers between devices: none -> 3.71 us  [per_device(): carries = lax.all_to_all(chains(devices)(edge), 'wa', 0, 0, tiled=True)]
    unnamed x10 -> x0, local copies, waits for them, and re-layouts: 3.48 us -> none
    all_to_all x0 -> x1, waiting for transfers between devices: none -> 3.33 us  [per_device(): carries = lax.all_to_all(chains(devices)(edge), 'wa', 0, 0, tiled=True)]
    pallas_call x2 -> x0, local copies, waits for them, and re-layouts: 1.39 us -> none  [per_device(): return unpacks()(lax.all_to_all(answer, 'ha', 0, 0, tiled=True))]
  transfers between devices with their start and end apart: 0 -> 1, of which waited for: 0 -> 1; matrix products, arithmetic and copies ran while one was open for 0% -> 0% of each run, Pallas kernels for 0% -> 8%
where the time goes in v2:
time: 98.6 us; the launch traced here: 98.3 us
  blocking collectives  69.1 us (70%)
  Pallas kernels  21.5 us (22%)
  starting transfers between devices  3.71 us (4%)
  waiting for transfers between devices  3.33 us (3%)
    all_to_all x1, blocking collectives, per_device(): tile = lax.all_to_all(message, 'ha', 0, 0, tiled=True)  28.5 us
    all_to_all x1, blocking collectives, per_device(): edge = lax.all_to_all(edge, 'wa', 0, 0, tiled=True)  22.3 us
    all_to_all x1, blocking collectives, per_device(): x, b, s, w, h = unpacks()(lax.all_to_all(answer, 'ha', 0, 0, tiled=True))  18.3 us
    pallas_call x1, Pallas kernels, per_device(): local, high, low = local_grads()(tile, back, place, table)  8.29 us
    pallas_call x1, Pallas kernels, per_device(): answer = outer_grads()(tile, carries, local, back, place, table, high, low)  5.49 us
    pallas_call x1, Pallas kernels, per_device(): edge, back, table, place = edges(devices)(tile)  3.75 us
    all_to_all x1, starting transfers between devices, per_device(): carries = lax.all_to_all(chains(devices)(edge), 'wa', 0, 0, tiled=True)  3.71 us
    all_to_all x1, waiting for transfers between devices, per_device(): carries = lax.all_to_all(chains(devices)(edge), 'wa', 0, 0, tiled=True)  3.33 us
  transfers between devices with their start and end apart: 1, of which 1 were waited for; matrix products, arithmetic and copies ran while one was open for 0% of the time, Pallas kernels for 8%

profile of v2, /device:TPU:1, one launch (start us, length us, event | category | flops | bytes accessed | tf_op | source)
XLA Modules:
  0.0 98.3 jit_solution(426478008443162379)
XLA Ops:
  0.6 2.2 %shard_map.101 = f32[8,168,128]{2,1,0:T(8,128)} custom-call(bf16[8,16,512]{2,1,0:T(8,128)(2,1)} %x0.1, bf16[8,16,512]{2,1,0:T(8,128)(2,1)} %y0.1, f32[8,16,16]{2,1,0:T(8,128)} %b0.1, f32[8,16,16]{2,1,0:T(8,128)} %s0.1, f32[8,8,16]{2,1,0:T(8,128)} %bitcast.4, f32[8,8,16]{2,1,0:T(8,128)} %bitcast.5), custom_call_target="tpu_custom_call" | custom-call | flops 100000000 | bytes 1000000 | tf_op jit(solution)/shard_map/pallas_call | solution.py:537
  2.8 28.5 %all_to_all.20.ref = f32[8,168,128]{2,1,0:T(8,128)S(1)} all-to-all(f32[8,168,128]{2,1,0:T(8,128)} %shard_map.101), channel_id=1, replica_groups=mesh['ha'=8,'wa'=32] {'ha'}, dimensions={0} | all-to-all | bytes 1376256 | tf_op jit(solution)/shard_map/all_to_all | solution.py:540
  31.3 3.7 %shard_map.102 = (f32[32,40,128]{2,1,0:T(8,128)S(1)}, f32[16,64,128]{2,1,0:T(8,128)S(1)}, f32[16,40,128]{2,1,0:T(8,128)S(1)}, bf16[8,128,256]{2,1,0:T(8,128)(2,1)S(1)}) custom-call(f32[8,168,128]{2,1,0:T(8,128)S(1)} %all_to_all.20.ref), custom_call_target="tpu_custom_call" | custom-call | flops 100000000 | bytes 1000000 | tf_op jit(solution)/shard_map/pallas_call | solution.py:541
  35.0 22.3 %all_to_all.21.got = f32[32,40,128]{2,1,0:T(8,128)S(1)} all-to-all(f32[32,40,128]{2,1,0:T(8,128)S(1)} %get-tuple-element.17), channel_id=1, replica_groups=mesh['ha'=8,'wa'=32] {'wa'}, dimensions={0} | all-to-all | bytes 1310720 | tf_op jit(solution)/shard_map/all_to_all | solution.py:542
  57.4 0.9 shard_map.103
  58.2 3.7 %all-to-all-start.2 = ((f32[32,32,128]{2,1,0:T(8,128)}), f32[32,32,128]{2,1,0:T(8,128)S(1)}, u32[]{:S(2)}, u32[]{:S(2)}) async-start(f32[32,32,128]{2,1,0:T(8,128)} %shard_map.103), calls=%async_computation.2 | async-start | bytes 1048576 | tf_op jit(solution)/shard_map/all_to_all | solution.py:544
  62.0 8.3 %shard_map.104 = (f32[8,104,128]{2,1,0:T(8,128)S(1)}, bf16[8,128,128]{2,1,0:T(8,128)(2,1)S(1)}, bf16[8,128,128]{2,1,0:T(8,128)(2,1)S(1)}) custom-call(f32[8,168,128]{2,1,0:T(8,128)S(1)} %all_to_all.20.ref, f32[16,64,128]{2,1,0:T(8,128)S(1)} %get-tuple-element.18.back, bf16[8,128,256]{2,1,0:T(8,128)(2,1)S(1)} %get-tuple-element.19.place, ...), custom_call_target="tpu_custom_call" | custom-call | flops 5000000000 | bytes 1000000 | tf_op jit(solution)/shard_map/pallas_call | solution.py:543
  70.3 3.3 %all-to-all-done.2.edge = f32[32,32,128]{2,1,0:T(8,128)S(1)} async-done(((f32[32,32,128]{2,1,0:T(8,128)}), f32[32,32,128]{2,1,0:T(8,128)S(1)}, u32[]{:S(2)}, u32[]{:S(2)}) %all-to-all-start.2) | async-done | bytes 524320 | tf_op jit(solution)/shard_map/all_to_all | solution.py:544
  73.6 5.5 %shard_map.105 = f32[8,104,128]{2,1,0:T(8,128)S(1)} custom-call(f32[8,168,128]{2,1,0:T(8,128)S(1)} %all_to_all.20.ref, f32[32,32,128]{2,1,0:T(8,128)S(1)} %all-to-all-done.2.edge, f32[8,104,128]{2,1,0:T(8,128)S(1)} %get-tuple-element.21.local, f32[16,64,128]{2,1,0:T(8,128)S(1)} %get-tuple-element.18.back, bf16[8,128,256]{2,1,0:T(8,128)(2,1)S(1)} %get-tuple-element.19.place, ...), custom_call_target="tpu_custom_call" | custom-call | flops 100000000 | bytes 1000000 | tf_op jit(solution)/shard_map/pallas_call | solution.py:545
  79.1 18.3 %all_to_all.22.got = f32[8,104,128]{2,1,0:T(8,128)S(1)} all-to-all(f32[8,104,128]{2,1,0:T(8,128)S(1)} %shard_map.105), channel_id=1, replica_groups=mesh['ha'=8,'wa'=32] {'ha'}, dimensions={0} | all-to-all | bytes 851968 | tf_op jit(solution)/shard_map/all_to_all | solution.py:546
  97.4 0.9 shard_map.106
Async XLA Ops:
  58.2 15.3 %all-to-all-start.2 = ((f32[32,32,128]{2,1,0:T(8,128)}), f32[32,32,128]{2,1,0:T(8,128)S(1)}, u32[]{:S(2)}, u32[]{:S(2)}) async-start(f32[32,32,128]{2,1,0:T(8,128)} %shard_map.103), calls=%async_computation.2 | async-start | bytes 1048576 | tf_op jit(solution)/shard_map/all_to_all | solution.py:544

commit v3 on v2

--- a/solution.py
+++ b/solution.py
@@ -19,12 +19,10 @@
 QUART = CH // STEP
 
 X0, C0, B0, S0, D0 = 0, 64, 128, 144, 160
-SENT = 168
+SENT = 162
 I0, O0, W0 = 64, 80, 96
-BACK = 104
-EDGE = 40
-UE, US, UF, UP = 2, 1, 1, 1
-PK = 60
+BACK = 98
+EDGE = 33
 
 
 def make_place(place):
@@ -42,6 +40,16 @@
     for col in range(COLS):
         hit = m == ((k % LANES) // N) * COLS + col
         gather[col] = jnp.where(hit, 1.0, 0.0).astype(BF16)
+
+
+def take(ref, at, size, count):
+    parts = [ref[g * count + at : g * count + at + size, :][None] for g in range(SEG)]
+    return jnp.concatenate(parts, axis=0)
+
+
+def give(ref, at, count, value):
+    for g in range(SEG):
+        ref[g * count + at : g * count + at + value.shape[1], :] = value[g]
 
 
 def pack_kernel(x0, y0, b0, s0, w0, h0, out, x, y, b, s, w, h, done):
@@ -52,53 +60,53 @@
     for copy in copies:
         copy.start()
     low = lax.broadcasted_iota(jnp.int32, (COLS, 128), 1) < CH
-    out[:, D0 + 2 :, :] = jnp.zeros((SEG, SENT - D0 - 2, 128), F32)
     for k, (at, a) in enumerate(((D0, w), (D0 + 1, h))):
         copies[k].wait()
         flat = jnp.concatenate([a[row] for row in range(ROWS)], axis=1)
         for g in range(SEG):
-            out[g, at : at + 1, :] = flat[g : g + 1]
+            out[g * SENT + at : g * SENT + at + 1, :] = flat[g : g + 1]
     for k, (at, a) in enumerate(((B0, b), (S0, s))):
         copies[2 + k].wait()
         flat = a[...].reshape(TOKENS, N).T
         for g in range(SEG):
-            out[g, at : at + N, :] = flat
+            out[g * SENT + at : g * SENT + at + N, :] = flat
     for k, (at, a) in enumerate(((X0, x), (C0, y))):
         copies[4 + k].wait()
         for pair in range(ROWS // 2):
-            rows = slice(at + pair * COLS, at + (pair + 1) * COLS)
+            to = at + pair * COLS
             for two in range(SEG // 2):
                 lanes = slice(two * 128, (two + 1) * 128)
                 one = a[2 * pair, :, lanes].astype(F32)
                 other = a[2 * pair + 1, :, lanes].astype(F32)
-                out[2 * two, rows, :] = jnp.where(low, one, pltpu.roll(other, CH, 1))
-                out[2 * two + 1, rows, :] = jnp.where(low, pltpu.roll(one, CH, 1), other)
+                even, odd = 2 * two * SENT + to, (2 * two + 1) * SENT + to
+                out[even : even + COLS, :] = jnp.where(low, one, pltpu.roll(other, CH, 1))
+                out[odd : odd + COLS, :] = jnp.where(low, pltpu.roll(one, CH, 1), other)
 
 
 def unpack_kernel(got, x, b, s, w, h):
     low = lax.broadcasted_iota(jnp.int32, (COLS, 128), 1) < CH
     for pair in range(ROWS // 2):
-        rows = slice(pair * COLS, (pair + 1) * COLS)
         for two in range(SEG // 2):
             lanes = slice(two * 128, (two + 1) * 128)
-            one = got[2 * two, rows, :]
-            other = got[2 * two + 1, rows, :]
+            even, odd = 2 * two * BACK + pair * COLS, (2 * two + 1) * BACK + pair * COLS
+            one = got[even : even + COLS, :]
+            other = got[odd : odd + COLS, :]
             x[2 * pair, :, lanes] = jnp.where(low, one, pltpu.roll(other, CH, 1))
             x[2 * pair + 1, :, lanes] = jnp.where(low, pltpu.roll(one, CH, 1), other)
     for at, a in ((I0, b), (O0, s)):
-        flat = got[0, at : at + N, :]
+        flat = got[at : at + N, :]
         for g in range(1, SEG):
-            flat = flat + got[g, at : at + N, :]
+            flat = flat + got[g * BACK + at : g * BACK + at + N, :]
         a[...] = flat.T.reshape(ROWS, COLS, N)
     for at, a in ((W0, w), (W0 + 1, h)):
-        flat = jnp.concatenate([got[g, at : at + 1, :] for g in range(SEG)], axis=0)
+        flat = jnp.concatenate([got[g * BACK + at : g * BACK + at + 1, :] for g in range(SEG)], axis=0)
         for row in range(ROWS):
             a[row] = flat[:, row * COLS : (row + 1) * COLS]
 
 
 def flip(ref, at, flipped):
     for pair in range(ROWS // 2):
-        block = ref[:, at + pair * COLS : at + (pair + 1) * COLS, :].reshape(SEG * COLS, 2 * CH)
+        block = take(ref, at + pair * COLS, COLS, SENT).reshape(SEG * COLS, 2 * CH)
         flipped[pair * 2 * CH : (pair + 1) * 2 * CH, :] = block.T.astype(BF16)
 
 
@@ -120,10 +128,10 @@
 
 def small(ref, flat, bt, ct, wr, hr):
     for at, out in ((B0, bt), (S0, ct)):
-        flat[...] = ref[:, at : at + N, :].reshape(LANES, TOKENS).T
+        flat[...] = take(ref, at, N, SENT).reshape(LANES, TOKENS).T
         by_column(flat, out)
     for at, out in ((D0, wr), (D0 + 1, hr)):
-        rate = jnp.exp(ref[:, at : at + 1, :])
+        rate = jnp.exp(take(ref, at, 1, SENT))
         flat[...] = jnp.broadcast_to(rate, (SEG, N, TOKENS)).reshape(LANES, TOKENS).T
         by_column(flat, out)
 
@@ -204,7 +212,7 @@
         back[col] = carry
         return none
 
-    lax.fori_loop(0, COLS, ends, 0, unroll=UE)
+    lax.fori_loop(0, COLS, ends, 0, unroll=2)
     carry_scan(back, rates, False)
 
     after = jnp.ones((ROWS, LANES), F32)
@@ -222,10 +230,9 @@
                 mine, low, preferred_element_type=F32
             )
             for q in range(QUART):
-                edge[row * QUART + q, 0:STEP, :] = tail[q * STEP : (q + 1) * STEP]
-                edge[row * QUART + q, 2 * STEP :, :] = jnp.broadcast_to(
-                    after[row : row + 1], (EDGE - 2 * STEP, LANES)
-                )
+                at = (row * QUART + q) * EDGE
+                edge[at : at + STEP, :] = tail[q * STEP : (q + 1) * STEP]
+                edge[at + 2 * STEP : at + EDGE, :] = after[row : row + 1]
 
     head[...] = jnp.zeros_like(head)
 
@@ -241,26 +248,23 @@
             head[row] = wr[col - 1, one, :] * (wr[col, one, :] * (head[row] + grad) + grad2)
         return none
 
-    lax.fori_loop(0, COLS // 2, sums, 0, unroll=US)
+    lax.fori_loop(0, COLS // 2, sums, 0)
     for row in range(ROWS):
         for q in range(QUART):
-            edge[row * QUART + q, STEP : 2 * STEP, :] = head[row, q * STEP : (q + 1) * STEP, :]
+            at = (row * QUART + q) * EDGE + STEP
+            edge[at : at + STEP, :] = head[row, q * STEP : (q + 1) * STEP, :]
 
 
 def chain_kernel(got, out):
-    count = got.shape[0]
-
-    def both(hop, carry):
-        right, left = carry
+    count = out.shape[0]
+    right = left = jnp.zeros((STEP, LANES), F32)
+    for hop in range(count):
         place = count - 1 - hop
         out[hop, 0:STEP, :] = right
         out[place, STEP : 2 * STEP, :] = left
-        right = got[hop, 2 * STEP : 2 * STEP + 1, :] * right + got[hop, 0:STEP, :]
-        left = got[place, 2 * STEP : 2 * STEP + 1, :] * left + got[place, STEP : 2 * STEP, :]
-        return right, left
-
-    zero = jnp.zeros((STEP, LANES), F32)
-    lax.fori_loop(0, count, both, (zero, zero), unroll=8)
+        one, other = hop * EDGE, place * EDGE
+        right = got[one + 2 * STEP : one + EDGE, :] * right + got[one : one + STEP, :]
+        left = got[other + 2 * STEP : other + EDGE, :] * left + got[other + STEP : other + 2 * STEP, :]
 
 
 def total8(v):
@@ -270,8 +274,8 @@
 
 
 def local_kernel(
-    ref, back, place, table, out, high, low,
-    gather, xe, ce, states, front, run, kept, pieces, sums, flipped, flat
+    ref, back, place, table, out, high, low, far_ce, far_grad,
+    gather, xe, ce, states, front, run, kept, pieces, sums, flipped, flat, done
 ):
     bt, ct, wr, hr, rates = tables(table)
     make_gather(gather)
@@ -288,6 +292,11 @@
     flip(ref, C0, flipped)
     for two in range(COLS // 2):
         spread(flipped, place, ce, two)
+    copies = [
+        pltpu.make_async_copy(source, target, done.at[k])
+        for k, (source, target) in enumerate(((ce, far_ce), (kept, far_grad)))
+    ]
+    copies[0].start()
     states[0] = jnp.zeros(BLOCK, F32)
     run[...] = jnp.zeros(BLOCK, F32)
 
@@ -301,7 +310,7 @@
         front[col] = total
         return none
 
-    lax.fori_loop(0, COLS, forward, 0, unroll=UF)
+    lax.fori_loop(0, COLS, forward, 0)
     carry_scan(front, rates, True)
 
     def products(step, none):
@@ -311,11 +320,11 @@
             one = slice(row, row + 1)
             grad = carry + ct[col, one, :] * ce[col, row]
             carry = hr[col, one, :] * grad
-            kept[row] = grad
+            kept[col, row] = grad
         total = front[col]
         for row in range(ROWS):
             one = slice(row, row + 1)
-            grad = kept[row]
+            grad = kept[col, row]
             sums[3, row, col] = total8(grad * total)
             total = hr[col, one, :] * total + states[col + 1, row]
             sums[1, row, col] = total8(total * ce[col, row])
@@ -328,16 +337,18 @@
             pieces[col, row * CH : (row + 1) * CH, LANES:] = low
         return none
 
-    lax.fori_loop(0, COLS, products, 0, unroll=UP)
+    lax.fori_loop(0, COLS, products, 0)
+    copies[1].start()
     for pair in range(ROWS // 2):
         rows = slice(pair * 2 * CH, (pair + 1) * 2 * CH)
         block = jnp.zeros((2 * CH, 128), F32)
         for col in range(COLS):
             block = block + jnp.dot(pieces[col, rows, :], gather[col], preferred_element_type=F32)
-        out[:, pair * COLS : (pair + 1) * COLS, :] = block.T.reshape(SEG, COLS, 2 * CH)
+        give(out, pair * COLS, BACK, block.T.reshape(SEG, COLS, 2 * CH))
     for which, at in enumerate((I0, O0, W0, W0 + 1)):
         put(ref, out, at, over_sublanes(sums.at[which]))
-    out[:, W0 + 2 :, :] = jnp.zeros((SEG, BACK - W0 - 2, 128), F32)
+    for copy in copies:
+        copy.wait()
 
 
 def over_sublanes(part):
@@ -352,17 +363,26 @@
     value = value.T.reshape(SEG, N, TOKENS)
     size = N
     if at >= W0:
-        rate = jnp.exp(ref[:, D0 + at - W0 : D0 + at - W0 + 1, :])
+        rate = jnp.exp(take(ref, D0 + at - W0, 1, SENT))
         value, size = rate * jnp.sum(value, axis=1, keepdims=True), 1
     if old is not None:
-        value = value + old[:, at : at + size, :]
-    out[:, at : at + size, :] = value
+        value = value + take(old, at, size, BACK)
+    give(out, at, BACK, value)
 
 
 def outer_kernel(
-    ref, edge, local, back, place, table, high, low, out,
-    before, after, ce, front, kept, sums, flipped, left, right, flat, raw, meet
+    ref, edge, local, table, high, low, far_ce, far_grad, out,
+    before, after, ce, inner, front, sums, left, right, flat, raw, meet, done
 ):
+    def fetch(col):
+        return (
+            pltpu.make_async_copy(far_grad.at[col], inner.at[col], done.at[0, col]),
+            pltpu.make_async_copy(far_ce.at[col], ce.at[col], done.at[1, col]),
+        )
+
+    for col in range(COLS):
+        for copy in fetch(col):
+            copy.start()
     bt, ct, wr, hr, rates = tables(table)
     value = jnp.ones((ROWS, LANES), F32)
     for col in range(COLS):
@@ -372,9 +392,6 @@
     for col in reversed(range(COLS)):
         after[col] = value
         value = value * wr[col]
-    flip(ref, C0, flipped)
-    for two in range(COLS // 2):
-        spread(flipped, place, ce, two)
     for row in range(ROWS):
         for q in range(QUART):
             part = slice(q * STEP, (q + 1) * STEP)
@@ -393,17 +410,14 @@
     carry_scan(front, rates, True)
 
     def products(col, none):
-        carry = back[col]
-        for row in reversed(range(ROWS)):
-            one = slice(row, row + 1)
-            grad = carry + ct[col, one, :] * ce[col, row]
-            carry = hr[col, one, :] * grad
-            kept[row] = grad
-            sums[2, row, col] = total8(grad * left[row])
+        for copy in fetch(col):
+            copy.wait()
         total = front[col]
         for row in range(ROWS):
             one = slice(row, row + 1)
-            sums[1, row, col] = total8(kept[row] * total)
+            grad = inner[col, row]
+            sums[2, row, col] = total8(grad * left[row])
+            sums[1, row, col] = total8(grad * total)
             total = hr[col, one, :] * total + before[col, one, :] * left[row]
             sums[0, row, col] = total8(total * ce[col, row])
         return none
@@ -414,8 +428,7 @@
     none = jnp.zeros((CH, LANES), BF16)
     half = lax.broadcasted_iota(jnp.int32, (LANES, 128), 1) < CH
     for pair in range(ROWS // 2):
-        rows = slice(pair * COLS, (pair + 1) * COLS)
-        tokens = ref[:, rows, :].reshape(SEG * COLS, 2 * CH).astype(BF16)
+        tokens = take(ref, X0 + pair * COLS, COLS, SENT).reshape(SEG * COLS, 2 * CH).astype(BF16)
         parts = [split(right[2 * pair + part]) for part in range(2)]
         both = [jnp.concatenate([parts[0][k], parts[1][k]], axis=0) for k in range(2)]
         found = []
@@ -435,7 +448,7 @@
                 )
             found.append(value)
         value = jnp.where(half, found[0], found[1]).reshape(SEG, COLS, 128)
-        out[:, rows, :] = local[:, rows, :] + value
+        give(out, pair * COLS, BACK, take(local, pair * COLS, COLS, BACK) + value)
 
     put(ref, out, O0, over_sublanes(sums.at[0]), local)
     put(ref, out, W0 + 1, over_sublanes(sums.at[1]), local)
@@ -460,7 +473,6 @@
         flat[pl.ds(col, ROWS, stride=COLS), :] = terms[col]
     put(ref, out, I0, raw[...], local)
     put(ref, out, W0, flat[...], local)
-    out[:, W0 + 2 :, :] = local[:, W0 + 2 :, :]
 
 
 WIDE = (COLS, ROWS, CH, LANES)
@@ -477,7 +489,8 @@
     return pltpu.VMEM(shape, kind)
 
 
-def call(kernel, ins, outs, scratch, mebibytes, kinds=None, place=pltpu.VMEM, flops=10**8):
+def call(kernel, ins, outs, scratch, mebibytes, kinds=None, place=pltpu.VMEM, flops=10**8, far_in=0, far_out=0):
+    near, far = pl.BlockSpec(memory_space=place), pl.BlockSpec(memory_space=pltpu.HBM)
     whole = pl.BlockSpec(memory_space=pltpu.VMEM)
     kinds = kinds or (F32,) * len(outs)
     shapes = tuple(jax.ShapeDtypeStruct(s, k) for s, k in zip(outs, kinds))
@@ -485,8 +498,8 @@
     return pl.pallas_call(
         kernel,
         out_shape=shapes[0] if single else shapes,
-        in_specs=[pl.BlockSpec(memory_space=place)] * ins,
-        out_specs=whole if single else (whole,) * len(outs),
+        in_specs=[near] * (ins - far_in) + [far] * far_in,
+        out_specs=whole if single else (whole,) * (len(outs) - far_out) + (far,) * far_out,
         scratch_shapes=scratch,
         compiler_params=pltpu.CompilerParams(vmem_limit_bytes=int(mebibytes * 1024 * 1024)),
         cost_estimate=pl.CostEstimate(flops=flops, bytes_accessed=10**6, transcendentals=0),
@@ -496,11 +509,11 @@
 def packs():
     scratch = [vm((ROWS, COLS, SEG * CH), BF16)] * 2 + [vm((ROWS, COLS, N))] * 2
     scratch += [vm((ROWS, SEG, COLS))] * 2 + [pltpu.SemaphoreType.DMA((6,))]
-    return call(pack_kernel, 6, [(SEG, SENT, 128)], scratch, PK, place=pltpu.HBM)
+    return call(pack_kernel, 6, [(SEG * SENT, 128)], scratch, 60, place=pltpu.HBM)
 
 
 def edges(devices):
-    outs = [(devices, EDGE, LANES), ENDS, TABLE, PLACE]
+    outs = [(devices * EDGE, LANES), ENDS, TABLE, PLACE]
     scratch = [vm(WIDE), vm((TOKENS, LANES)), vm(RATES), vm(BLOCK), vm(FLIP, BF16)]
     return call(edges_kernel, 1, outs, scratch, 14, kinds=(F32, F32, F32, BF16))
 
@@ -510,22 +523,28 @@
 
 
 def local_grads():
-    outs = [(SEG, BACK, 128), (ROWS, LANES, LANES), (ROWS, LANES, LANES)]
+    outs = [(SEG * BACK, 128), (ROWS, LANES, LANES), (ROWS, LANES, LANES), WIDE, WIDE]
     scratch = [vm((COLS, 2 * LANES, 128), BF16), vm(WIDE), vm(WIDE), vm((COLS + 1,) + BLOCK), vm(ENDS)]
-    scratch += [vm(BLOCK), vm(BLOCK), vm((COLS, ROWS * CH, 2 * LANES), BF16), vm((4, ROWS, COLS, 8, LANES))]
-    scratch += [vm(FLIP, BF16), vm((TOKENS, LANES))]
-    return call(local_kernel, 4, outs, scratch, 28, kinds=(F32, BF16, BF16), flops=5 * 10**9)
+    scratch += [vm(BLOCK), vm(WIDE), vm((COLS, ROWS * CH, 2 * LANES), BF16), vm((4, ROWS, COLS, 8, LANES))]
+    scratch += [vm(FLIP, BF16), vm((TOKENS, LANES)), pltpu.SemaphoreType.DMA((2,))]
+    kinds = (F32, BF16, BF16, F32, F32)
+    return call(local_kernel, 4, outs, scratch, 50, kinds=kinds, flops=5 * 10**9, far_out=2)
 
 
 def outer_grads():
-    scratch = [vm(TOKEN), vm(TOKEN), vm(WIDE), vm(ENDS), vm(BLOCK), vm((3, ROWS, COLS, 8, LANES))]
-    scratch += [vm(FLIP, BF16), vm(BLOCK), vm(BLOCK), vm((TOKENS, LANES)), vm((TOKENS, LANES)), vm((ROWS, LANES))]
-    return call(outer_kernel, 8, [(SEG, BACK, 128)], scratch, 16)
+    scratch = [vm(TOKEN), vm(TOKEN), vm(WIDE), vm(WIDE), vm(ENDS), vm((3, ROWS, COLS, 8, LANES)), vm(BLOCK)]
+    scratch += [vm(BLOCK), vm((TOKENS, LANES)), vm((TOKENS, LANES)), vm((ROWS, LANES))]
+    scratch += [pltpu.SemaphoreType.DMA((2, COLS))]
+    return call(outer_kernel, 8, [(SEG * BACK, 128)], scratch, 50, far_in=2)
 
 
 def unpacks():
     outs = [(ROWS, COLS, SEG * CH)] + [(ROWS, COLS, N)] * 2 + [(ROWS, SEG, COLS)] * 2
     return call(unpack_kernel, 1, outs, [], 8)
+
+
+def exchange(a, axis):
+    return lax.all_to_all(a.reshape(-1, 1, LANES), axis, 0, 0, tiled=True).reshape(-1, LANES)
 
 
 def swapped(a):
@@ -537,13 +556,13 @@
     message = packs()(
         tokens, cotangent, state_in, state_out, swapped(width_decay), swapped(height_decay)
     )
-    tile = lax.all_to_all(message, "ha", 0, 0, tiled=True)
+    tile = exchange(message, "ha")
     edge, back, table, place = edges(devices)(tile)
-    edge = lax.all_to_all(edge, "wa", 0, 0, tiled=True)
-    local, high, low = local_grads()(tile, back, place, table)
+    edge = exchange(edge, "wa")
+    local, high, low, *far = local_grads()(tile, back, place, table)
     carries = lax.all_to_all(chains(devices)(edge), "wa", 0, 0, tiled=True)
-    answer = outer_grads()(tile, carries, local, back, place, table, high, low)
-    x, b, s, w, h = unpacks()(lax.all_to_all(answer, "ha", 0, 0, tiled=True))
+    answer = outer_grads()(tile, carries, local, table, high, low, *far)
+    x, b, s, w, h = unpacks()(exchange(answer, "ha"))
     return x, b, s, swapped(w), swapped(h)
 
 

time: 98.6 us -> 95.7 us (0.971)
  blocking collectives: 69.1 us -> 66.9 us
    all_to_all x3, blocking collectives: 69.1 us -> 66.9 us  [exchange(): lax.all_to_all(a.reshape(-1, 1, LANES), axis, 0, 0, tiled=True)]
  transfers between devices with their start and end apart: 1 -> 1, of which waited for: 1 -> 1; matrix products, arithmetic and copies ran while one was open for 0% -> 0% of each run, Pallas kernels for 8% -> 9%
where the time goes in v3:
time: 95.7 us; the launch traced here: 95.4 us
  blocking collectives  66.9 us (70%)
  Pallas kernels  21.4 us (22%)
  starting transfers between devices  3.68 us (4%)
  waiting for transfers between devices  2.73 us (3%)
    all_to_all x3, blocking collectives, exchange(): lax.all_to_all(a.reshape(-1, 1, LANES), axis, 0, 0, tiled=True)  66.9 us
    pallas_call x1, Pallas kernels, per_device(): local, high, low, *far = local_grads()(tile, back, place, table)  8.84 us
    pallas_call x1, Pallas kernels, per_device(): answer = outer_grads()(tile, carries, local, table, high, low, *far)  4.8 us
    pallas_call x1, Pallas kernels, per_device(): edge, back, table, place = edges(devices)(tile)  3.75 us
    all_to_all x1, starting transfers between devices, per_device(): carries = lax.all_to_all(chains(devices)(edge), 'wa', 0, 0, tiled=True)  3.68 us
    all_to_all x1, waiting for transfers between devices, per_device(): carries = lax.all_to_all(chains(devices)(edge), 'wa', 0, 0, tiled=True)  2.73 us
    pallas_call x1, Pallas kernels, per_device(): packs()  2.17 us
  transfers between devices with their start and end apart: 1, of which 1 were waited for; matrix products, arithmetic and copies ran while one was open for 0% of the time, Pallas kernels for 9%

profile of v3, /device:TPU:1, one launch (start us, length us, event | category | flops | bytes accessed | tf_op | source)
XLA Modules:
  0.0 95.4 jit_solution(10795819671338552755)
XLA Ops:
  0.6 2.2 %shard_map.101 = f32[1296,128]{1,0:T(8,128)} custom-call(bf16[8,16,512]{2,1,0:T(8,128)(2,1)} %x0.1, bf16[8,16,512]{2,1,0:T(8,128)(2,1)} %y0.1, f32[8,16,16]{2,1,0:T(8,128)} %b0.1, f32[8,16,16]{2,1,0:T(8,128)} %s0.1, f32[8,8,16]{2,1,0:T(8,128)} %bitcast.24, f32[8,8,16]{2,1,0:T(8,128)} %bitcast.25), custom_call_target="tpu_custom_call" | custom-call | flops 100000000 | bytes 1000000 | tf_op jit(solution)/shard_map/pallas_call | solution.py:556
  2.8 28.3 %all_to_all.20 = f32[1296,1,128]{2,1,0:T(1,128)S(1)} all-to-all(f32[1296,1,128]{2,1,0:T(1,128)} %bitcast.23), channel_id=1, replica_groups=mesh['ha'=8,'wa'=32] {'ha'}, dimensions={0} | all-to-all | bytes 1327104 | tf_op jit(solution)/shard_map/all_to_all | solution.py:547
  31.1 3.7 %shard_map.102 = (f32[1056,128]{1,0:T(8,128)S(1)}, f32[16,64,128]{2,1,0:T(8,128)S(1)}, f32[16,40,128]{2,1,0:T(8,128)S(1)}, bf16[8,128,256]{2,1,0:T(8,128)(2,1)S(1)}) custom-call(f32[1296,128]{1,0:T(8,128)S(1)} %bitcast.16), custom_call_target="tpu_custom_call" | custom-call | flops 100000000 | bytes 1000000 | tf_op jit(solution)/shard_map/pallas_call | solution.py:560
  34.9 20.8 %all_to_all.21 = f32[1056,1,128]{2,1,0:T(1,128)S(1)} all-to-all(f32[1056,1,128]{2,1,0:T(1,128)S(1)} %bitcast.22), channel_id=1, replica_groups=mesh['ha'=8,'wa'=32] {'wa'}, dimensions={0} | all-to-all | bytes 1081344 | tf_op jit(solution)/shard_map/all_to_all | solution.py:547
  55.7 0.9 shard_map.103
  56.6 3.7 %all-to-all-start.2 = ((f32[32,32,128]{2,1,0:T(8,128)}), f32[32,32,128]{2,1,0:T(8,128)S(1)}, u32[]{:S(2)}, u32[]{:S(2)}) async-start(f32[32,32,128]{2,1,0:T(8,128)} %shard_map.103), calls=%async_computation.2 | async-start | bytes 1048576 | tf_op jit(solution)/shard_map/all_to_all | solution.py:563
  60.3 8.8 %shard_map.104 = (f32[784,128]{1,0:T(8,128)S(1)}, bf16[8,128,128]{2,1,0:T(8,128)(2,1)S(1)}, bf16[8,128,128]{2,1,0:T(8,128)(2,1)S(1)}, f32[16,8,64,128]{3,2,1,0:T(8,128)}, f32[16,8,64,128]{3,2,1,0:T(8,128)}) custom-call(f32[1296,128]{1,0:T(8,128)S(1)} %bitcast.17, f32[16,64,128]{2,1,0:T(8,128)S(1)} %get-tuple-element.20.back, ...), custom_call_target="tpu_custom_call" | custom-call | flops 5000000000 | bytes 1000000 | tf_op jit(solution)/shard_map/pallas_call | solution.py:562
  69.1 2.7 %all-to-all-done.2.edge = f32[32,32,128]{2,1,0:T(8,128)S(1)} async-done(((f32[32,32,128]{2,1,0:T(8,128)}), f32[32,32,128]{2,1,0:T(8,128)S(1)}, u32[]{:S(2)}, u32[]{:S(2)}) %all-to-all-start.2) | async-done | bytes 524320 | tf_op jit(solution)/shard_map/all_to_all | solution.py:563
  71.9 4.8 %shard_map.105 = f32[784,128]{1,0:T(8,128)S(1)} custom-call(f32[1296,128]{1,0:T(8,128)S(1)} %bitcast.18, f32[32,32,128]{2,1,0:T(8,128)S(1)} %all-to-all-done.2.edge, f32[784,128]{1,0:T(8,128)S(1)} %get-tuple-element.23.local, f32[16,40,128]{2,1,0:T(8,128)S(1)} %get-tuple-element.22.table, bf16[8,128,128]{2,1,0:T(8,128)(2,1)S(1)} %get-tuple-element.24.high, ...), custom_call_target="tpu_custom_call" | custom-call | flops 100000000 | bytes 1000000 | tf_op jit(solution)/shard_map/pallas_call | solution.py:564
  76.7 17.8 %all_to_all.22 = f32[784,1,128]{2,1,0:T(1,128)S(1)} all-to-all(f32[784,1,128]{2,1,0:T(1,128)S(1)} %bitcast.20), channel_id=1, replica_groups=mesh['ha'=8,'wa'=32] {'ha'}, dimensions={0} | all-to-all | bytes 802816 | tf_op jit(solution)/shard_map/all_to_all | solution.py:547
  94.5 0.9 shard_map.106
Async XLA Ops:
  56.6 15.3 %all-to-all-start.2 = ((f32[32,32,128]{2,1,0:T(8,128)}), f32[32,32,128]{2,1,0:T(8,128)S(1)}, u32[]{:S(2)}, u32[]{:S(2)}) async-start(f32[32,32,128]{2,1,0:T(8,128)} %shard_map.103), calls=%async_computation.2 | async-start | bytes 1048576 | tf_op jit(solution)/shard_map/all_to_all | solution.py:563

commit v4 on v3

--- a/solution.py
+++ b/solution.py
@@ -110,15 +110,16 @@
         flipped[pair * 2 * CH : (pair + 1) * 2 * CH, :] = block.T.astype(BF16)
 
 
-def spread(flipped, place, wide, two):
+def spread(flipped, place, wide, two, thin=None):
     for pair in range(ROWS // 2):
         block = flipped[pair * 2 * CH : (pair + 1) * 2 * CH, :]
         out = jnp.dot(block, place[two], preferred_element_type=F32)
         for part in range(2):
             for half in range(2):
-                wide[2 * two + half, 2 * pair + part] = out[
-                    part * CH : (part + 1) * CH, half * LANES : (half + 1) * LANES
-                ]
+                value = out[part * CH : (part + 1) * CH, half * LANES : (half + 1) * LANES]
+                wide[2 * two + half, 2 * pair + part] = value
+                if thin is not None:
+                    thin[2 * two + half, 2 * pair + part] = value.astype(BF16)
 
 
 def by_column(flat, out):
@@ -168,14 +169,14 @@
     move = mover(down)
     keep = inside(down)
 
-    def column(col, none):
-        f = jnp.where(keep, move(ends[col], 1), 0.0)
+    for part in range(2):
+        cols = range(part * COLS // 2, (part + 1) * COLS // 2)
+        values = [jnp.where(keep, move(ends[col], 1), 0.0) for col in cols]
         for k, by in enumerate((1, 2, 4)):
-            f = f + rates[col, k : k + 1, :] * move(f, by)
-        ends[col] = f
-        return none
-
-    lax.fori_loop(0, COLS, column, 0, unroll=4)
+            moved = [move(f, by) for f in values]
+            values = [f + rates[col, k : k + 1, :] * g for col, f, g in zip(cols, values, moved)]
+        for col, f in zip(cols, values):
+            ends[col] = f
 
 
 def split(v):
@@ -204,15 +205,17 @@
     for two in range(COLS // 2):
         spread(flipped, place, ce, two)
 
-    def ends(col, none):
-        carry = jnp.zeros((CH, LANES), F32)
+    def ends(step, none):
+        cols = [step * 4 + k for k in range(4)]
+        carries = [jnp.zeros((CH, LANES), F32)] * 4
         for row in reversed(range(ROWS)):
             one = slice(row, row + 1)
-            carry = hr[col, one, :] * (carry + ct[col, one, :] * ce[col, row])
-        back[col] = carry
+            carries = [hr[c, one, :] * (v + ct[c, one, :] * ce[c, row]) for c, v in zip(cols, carries)]
+        for c, v in zip(cols, carries):
+            back[c] = v
         return none
 
-    lax.fori_loop(0, COLS, ends, 0, unroll=2)
+    lax.fori_loop(0, COLS // 4, ends, 0)
     carry_scan(back, rates, False)
 
     after = jnp.ones((ROWS, LANES), F32)
@@ -275,7 +278,7 @@
 
 def local_kernel(
     ref, back, place, table, out, high, low, far_ce, far_grad,
-    gather, xe, ce, states, front, run, kept, pieces, sums, flipped, flat, done
+    gather, xe, ce, states, front, run, kept, pieces, sums, flipped, flat, thin, done
 ):
     bt, ct, wr, hr, rates = tables(table)
     make_gather(gather)
@@ -291,10 +294,10 @@
         spread(flipped, place, xe, two)
     flip(ref, C0, flipped)
     for two in range(COLS // 2):
-        spread(flipped, place, ce, two)
+        spread(flipped, place, ce, two, thin)
     copies = [
         pltpu.make_async_copy(source, target, done.at[k])
-        for k, (source, target) in enumerate(((ce, far_ce), (kept, far_grad)))
+        for k, (source, target) in enumerate(((thin, far_ce), (kept, far_grad)))
     ]
     copies[0].start()
     states[0] = jnp.zeros(BLOCK, F32)
@@ -398,34 +401,8 @@
             left[row, part, :] = edge[row * QUART + q, 0:STEP, :]
             right[row, part, :] = edge[row * QUART + q, STEP : 2 * STEP, :]
 
-    def forward(col, none):
-        total = jnp.zeros((CH, LANES), F32)
-        for row in range(ROWS):
-            one = slice(row, row + 1)
-            total = hr[col, one, :] * total + before[col, one, :] * left[row]
-        front[col] = total
-        return none
-
-    lax.fori_loop(0, COLS, forward, 0)
-    carry_scan(front, rates, True)
-
-    def products(col, none):
-        for copy in fetch(col):
-            copy.wait()
-        total = front[col]
-        for row in range(ROWS):
-            one = slice(row, row + 1)
-            grad = inner[col, row]
-            sums[2, row, col] = total8(grad * left[row])
-            sums[1, row, col] = total8(grad * total)
-            total = hr[col, one, :] * total + before[col, one, :] * left[row]
-            sums[0, row, col] = total8(total * ce[col, row])
-        return none
-
-    lax.fori_loop(0, COLS, products, 0)
-
     own = own_segment()
-    none = jnp.zeros((CH, LANES), BF16)
+    empty = jnp.zeros((CH, LANES), BF16)
     half = lax.broadcasted_iota(jnp.int32, (LANES, 128), 1) < CH
     for pair in range(ROWS // 2):
         tokens = take(ref, X0 + pair * COLS, COLS, SENT).reshape(SEG * COLS, 2 * CH).astype(BF16)
@@ -436,7 +413,7 @@
             row = 2 * pair + part
             value = jnp.zeros((LANES, LANES), F32)
             for k in range(2):
-                pieces = [parts[0][k], none] if part == 0 else [none, parts[1][k]]
+                pieces = [parts[0][k], empty] if part == 0 else [empty, parts[1][k]]
                 value = value + jnp.dot(tokens, jnp.concatenate(pieces, axis=0), preferred_element_type=F32)
             value = jnp.where(own, value, 0.0).reshape(SEG, COLS, LANES)
             raw[row * COLS : (row + 1) * COLS, :] = jnp.sum(value, axis=0)
@@ -449,6 +426,35 @@
             found.append(value)
         value = jnp.where(half, found[0], found[1]).reshape(SEG, COLS, 128)
         give(out, pair * COLS, BACK, take(local, pair * COLS, COLS, BACK) + value)
+
+    def forward(step, none):
+        cols = [step * 4 + k for k in range(4)]
+        totals = [jnp.zeros((CH, LANES), F32)] * 4
+        for row in range(ROWS):
+            one = slice(row, row + 1)
+            enter = left[row]
+            totals = [hr[c, one, :] * v + before[c, one, :] * enter for c, v in zip(cols, totals)]
+        for c, v in zip(cols, totals):
+            front[c] = v
+        return none
+
+    lax.fori_loop(0, COLS // 4, forward, 0)
+    carry_scan(front, rates, True)
+
+    def products(col, none):
+        for copy in fetch(col):
+            copy.wait()
+        total = front[col]
+        for row in range(ROWS):
+            one = slice(row, row + 1)
+            grad = inner[col, row]
+            sums[2, row, col] = total8(grad * left[row])
+            sums[1, row, col] = total8(grad * total)
+            total = hr[col, one, :] * total + before[col, one, :] * left[row]
+            sums[0, row, col] = total8(total * ce[col, row].astype(F32))
+        return none
+
+    lax.fori_loop(0, COLS, products, 0)
 
     put(ref, out, O0, over_sublanes(sums.at[0]), local)
     put(ref, out, W0 + 1, over_sublanes(sums.at[1]), local)
@@ -526,13 +532,13 @@
     outs = [(SEG * BACK, 128), (ROWS, LANES, LANES), (ROWS, LANES, LANES), WIDE, WIDE]
     scratch = [vm((COLS, 2 * LANES, 128), BF16), vm(WIDE), vm(WIDE), vm((COLS + 1,) + BLOCK), vm(ENDS)]
     scratch += [vm(BLOCK), vm(WIDE), vm((COLS, ROWS * CH, 2 * LANES), BF16), vm((4, ROWS, COLS, 8, LANES))]
-    scratch += [vm(FLIP, BF16), vm((TOKENS, LANES)), pltpu.SemaphoreType.DMA((2,))]
-    kinds = (F32, BF16, BF16, F32, F32)
+    scratch += [vm(FLIP, BF16), vm((TOKENS, LANES)), vm(WIDE, BF16), pltpu.SemaphoreType.DMA((2,))]
+    kinds = (F32, BF16, BF16, BF16, F32)
     return call(local_kernel, 4, outs, scratch, 50, kinds=kinds, flops=5 * 10**9, far_out=2)
 
 
 def outer_grads():
-    scratch = [vm(TOKEN), vm(TOKEN), vm(WIDE), vm(WIDE), vm(ENDS), vm((3, ROWS, COLS, 8, LANES)), vm(BLOCK)]
+    scratch = [vm(TOKEN), vm(TOKEN), vm(WIDE, BF16), vm(WIDE), vm(ENDS), vm((3, ROWS, COLS, 8, LANES)), vm(BLOCK)]
     scratch += [vm(BLOCK), vm((TOKENS, LANES)), vm((TOKENS, LANES)), vm((ROWS, LANES))]
     scratch += [pltpu.SemaphoreType.DMA((2, COLS))]
     return call(outer_kernel, 8, [(SEG * BACK, 128)], scratch, 50, far_in=2)

time: 95.7 us -> 93.9 us (0.981)
  Pallas kernels: 21.4 us -> 18.9 us
    pallas_call x1, Pallas kernels: 3.75 us -> 2.76 us  [per_device(): edge, back, table, place = edges(devices)(tile)]
where the time goes in v4:
time: 93.9 us; the launch traced here: 93.6 us
  blocking collectives  66.9 us (71%)
  Pallas kernels  18.9 us (20%)
  starting transfers between devices  3.68 us (4%)
  waiting for transfers between devices  3.38 us (4%)
    all_to_all x3, blocking collectives, exchange(): lax.all_to_all(a.reshape(-1, 1, LANES), axis, 0, 0, tiled=True)  66.9 us
    pallas_call x1, Pallas kernels, per_device(): local, high, low, *far = local_grads()(tile, back, place, table)  8.19 us
    pallas_call x1, Pallas kernels, per_device(): answer = outer_grads()(tile, carries, local, table, high, low, *far)  4.03 us
    all_to_all x1, starting transfers between devices, per_device(): carries = lax.all_to_all(chains(devices)(edge), 'wa', 0, 0, tiled=True)  3.68 us
    all_to_all x1, waiting for transfers between devices, per_device(): carries = lax.all_to_all(chains(devices)(edge), 'wa', 0, 0, tiled=True)  3.38 us
    pallas_call x1, Pallas kernels, per_device(): edge, back, table, place = edges(devices)(tile)  2.76 us
    pallas_call x1, Pallas kernels, per_device(): packs()  2.17 us
  transfers between devices with their start and end apart: 1, of which 1 were waited for; matrix products, arithmetic and copies ran while one was open for 0% of the time, Pallas kernels for 9%

profile of v4, /device:TPU:1, one launch (start us, length us, event | category | flops | bytes accessed | tf_op | source)
XLA Modules:
  0.0 93.6 jit_solution(16935470803242742819)
XLA Ops:
  0.6 2.2 %shard_map.101 = f32[1296,128]{1,0:T(8,128)} custom-call(bf16[8,16,512]{2,1,0:T(8,128)(2,1)} %x0.1, bf16[8,16,512]{2,1,0:T(8,128)(2,1)} %y0.1, f32[8,16,16]{2,1,0:T(8,128)} %b0.1, f32[8,16,16]{2,1,0:T(8,128)} %s0.1, f32[8,8,16]{2,1,0:T(8,128)} %bitcast.24, f32[8,8,16]{2,1,0:T(8,128)} %bitcast.25), custom_call_target="tpu_custom_call" | custom-call | flops 100000000 | bytes 1000000 | tf_op jit(solution)/shard_map/pallas_call | solution.py:562
  2.8 28.3 %all_to_all.20 = f32[1296,1,128]{2,1,0:T(1,128)S(1)} all-to-all(f32[1296,1,128]{2,1,0:T(1,128)} %bitcast.23), channel_id=1, replica_groups=mesh['ha'=8,'wa'=32] {'ha'}, dimensions={0} | all-to-all | bytes 1327104 | tf_op jit(solution)/shard_map/all_to_all | solution.py:553
  31.1 2.8 %shard_map.102 = (f32[1056,128]{1,0:T(8,128)S(1)}, f32[16,64,128]{2,1,0:T(8,128)S(1)}, f32[16,40,128]{2,1,0:T(8,128)S(1)}, bf16[8,128,256]{2,1,0:T(8,128)(2,1)S(1)}) custom-call(f32[1296,128]{1,0:T(8,128)S(1)} %bitcast.16), custom_call_target="tpu_custom_call" | custom-call | flops 100000000 | bytes 1000000 | tf_op jit(solution)/shard_map/pallas_call | solution.py:566
  33.9 20.8 %all_to_all.21 = f32[1056,1,128]{2,1,0:T(1,128)S(1)} all-to-all(f32[1056,1,128]{2,1,0:T(1,128)S(1)} %bitcast.22), channel_id=1, replica_groups=mesh['ha'=8,'wa'=32] {'wa'}, dimensions={0} | all-to-all | bytes 1081344 | tf_op jit(solution)/shard_map/all_to_all | solution.py:553
  54.7 0.9 shard_map.103
  55.6 3.7 %all-to-all-start.2 = ((f32[32,32,128]{2,1,0:T(8,128)}), f32[32,32,128]{2,1,0:T(8,128)S(1)}, u32[]{:S(2)}, u32[]{:S(2)}) async-start(f32[32,32,128]{2,1,0:T(8,128)} %shard_map.103), calls=%async_computation.2 | async-start | bytes 1048576 | tf_op jit(solution)/shard_map/all_to_all | solution.py:569
  59.3 8.2 %shard_map.104 = (f32[784,128]{1,0:T(8,128)S(1)}, bf16[8,128,128]{2,1,0:T(8,128)(2,1)S(1)}, bf16[8,128,128]{2,1,0:T(8,128)(2,1)S(1)}, bf16[16,8,64,128]{3,2,1,0:T(8,128)(2,1)}, f32[16,8,64,128]{3,2,1,0:T(8,128)}) custom-call(f32[1296,128]{1,0:T(8,128)S(1)} %bitcast.17, f32[16,64,128]{2,1,0:T(8,128)S(1)} %get-tuple-element.20.back, ...), custom_call_target="tpu_custom_call" | custom-call | flops 5000000000 | bytes 1000000 | tf_op jit(solution)/shard_map/pallas_call | solution.py:568
  67.5 3.4 %all-to-all-done.2.edge = f32[32,32,128]{2,1,0:T(8,128)S(1)} async-done(((f32[32,32,128]{2,1,0:T(8,128)}), f32[32,32,128]{2,1,0:T(8,128)S(1)}, u32[]{:S(2)}, u32[]{:S(2)}) %all-to-all-start.2) | async-done | bytes 524320 | tf_op jit(solution)/shard_map/all_to_all | solution.py:569
  70.8 4.0 %shard_map.105 = f32[784,128]{1,0:T(8,128)S(1)} custom-call(f32[1296,128]{1,0:T(8,128)S(1)} %bitcast.18, f32[32,32,128]{2,1,0:T(8,128)S(1)} %all-to-all-done.2.edge, f32[784,128]{1,0:T(8,128)S(1)} %get-tuple-element.23.local, f32[16,40,128]{2,1,0:T(8,128)S(1)} %get-tuple-element.22.table, bf16[8,128,128]{2,1,0:T(8,128)(2,1)S(1)} %get-tuple-element.24.high, ...), custom_call_target="tpu_custom_call" | custom-call | flops 100000000 | bytes 1000000 | tf_op jit(solution)/shard_map/pallas_call | solution.py:570
  74.9 17.8 %all_to_all.22 = f32[784,1,128]{2,1,0:T(1,128)S(1)} all-to-all(f32[784,1,128]{2,1,0:T(1,128)S(1)} %bitcast.21), channel_id=1, replica_groups=mesh['ha'=8,'wa'=32] {'ha'}, dimensions={0} | all-to-all | bytes 802816 | tf_op jit(solution)/shard_map/all_to_all | solution.py:553
  92.7 0.9 shard_map.106
Async XLA Ops:
  55.6 15.3 %all-to-all-start.2 = ((f32[32,32,128]{2,1,0:T(8,128)}), f32[32,32,128]{2,1,0:T(8,128)S(1)}, u32[]{:S(2)}, u32[]{:S(2)}) async-start(f32[32,32,128]{2,1,0:T(8,128)} %shard_map.103), calls=%async_computation.2 | async-start | bytes 1048576 | tf_op jit(solution)/shard_map/all_to_all | solution.py:569

commit v5 on v4

--- a/solution.py
+++ b/solution.py
@@ -210,7 +210,10 @@
         carries = [jnp.zeros((CH, LANES), F32)] * 4
         for row in reversed(range(ROWS)):
             one = slice(row, row + 1)
-            carries = [hr[c, one, :] * (v + ct[c, one, :] * ce[c, row]) for c, v in zip(cols, carries)]
+            seeded = [ct[c, one, :] * ce[c, row] for c in cols]
+            for c, v in zip(cols, seeded):
+                ce[c, row] = v
+            carries = [hr[c, one, :] * (v + seed) for c, v, seed in zip(cols, carries, seeded)]
         for c, v in zip(cols, carries):
             back[c] = v
         return none
@@ -244,9 +247,9 @@
         carry, carry2 = back[col], back[col - 1]
         for row in reversed(range(ROWS)):
             one = slice(row, row + 1)
-            grad = carry + ct[col, one, :] * ce[col, row]
+            grad = carry + ce[col, row]
             carry = hr[col, one, :] * grad
-            grad2 = carry2 + ct[col - 1, one, :] * ce[col - 1, row]
+            grad2 = carry2 + ce[col - 1, row]
             carry2 = hr[col - 1, one, :] * grad2
             head[row] = wr[col - 1, one, :] * (wr[col, one, :] * (head[row] + grad) + grad2)
         return none
@@ -375,7 +378,7 @@
 
 def outer_kernel(
     ref, edge, local, table, high, low, far_ce, far_grad, out,
-    before, after, ce, inner, front, sums, left, right, flat, raw, meet, done
+    before, after, ce, inner, front, sums, left, right, flat, raw, meet, entered, done
 ):
     def fetch(col):
         return (
@@ -433,7 +436,10 @@
         for row in range(ROWS):
             one = slice(row, row + 1)
             enter = left[row]
-            totals = [hr[c, one, :] * v + before[c, one, :] * enter for c, v in zip(cols, totals)]
+            parts = [before[c, one, :] * enter for c in cols]
+            for c, v in zip(cols, parts):
+                entered[c, row] = v
+            totals = [hr[c, one, :] * v + part for c, v, part in zip(cols, totals, parts)]
         for c, v in zip(cols, totals):
             front[c] = v
         return none
@@ -450,7 +456,7 @@
             grad = inner[col, row]
             sums[2, row, col] = total8(grad * left[row])
             sums[1, row, col] = total8(grad * total)
-            total = hr[col, one, :] * total + before[col, one, :] * left[row]
+            total = hr[col, one, :] * total + entered[col, row]
             sums[0, row, col] = total8(total * ce[col, row].astype(F32))
         return none
 
@@ -540,7 +546,7 @@
 def outer_grads():
     scratch = [vm(TOKEN), vm(TOKEN), vm(WIDE, BF16), vm(WIDE), vm(ENDS), vm((3, ROWS, COLS, 8, LANES)), vm(BLOCK)]
     scratch += [vm(BLOCK), vm((TOKENS, LANES)), vm((TOKENS, LANES)), vm((ROWS, LANES))]
-    scratch += [pltpu.SemaphoreType.DMA((2, COLS))]
+    scratch += [vm(WIDE), pltpu.SemaphoreType.DMA((2, COLS))]
     return call(outer_kernel, 8, [(SEG * BACK, 128)], scratch, 50, far_in=2)
 
 

time: 93.9 us -> 93.8 us (level)
  no operation moved by 1% of the time
where the time goes in v5:
time: 93.8 us; the launch traced here: 93.4 us
  blocking collectives  66.9 us (71%)
  Pallas kernels  18.8 us (20%)
  starting transfers between devices  3.68 us (4%)
  waiting for transfers between devices  3.38 us (4%)
    all_to_all x3, blocking collectives, exchange(): lax.all_to_all(a.reshape(-1, 1, LANES), axis, 0, 0, tiled=True)  66.9 us
    pallas_call x1, Pallas kernels, per_device(): local, high, low, *far = local_grads()(tile, back, place, table)  8.19 us
    pallas_call x1, Pallas kernels, per_device(): answer = outer_grads()(tile, carries, local, table, high, low, *far)  3.99 us
    all_to_all x1, starting transfers between devices, per_device(): carries = lax.all_to_all(chains(devices)(edge), 'wa', 0, 0, tiled=True)  3.68 us
    all_to_all x1, waiting for transfers between devices, per_device(): carries = lax.all_to_all(chains(devices)(edge), 'wa', 0, 0, tiled=True)  3.38 us
    pallas_call x1, Pallas kernels, per_device(): edge, back, table, place = edges(devices)(tile)  2.63 us
    pallas_call x1, Pallas kernels, per_device(): packs()  2.17 us
  transfers between devices with their start and end apart: 1, of which 1 were waited for; matrix products, arithmetic and copies ran while one was open for 0% of the time, Pallas kernels for 9%

profile of v5, /device:TPU:1, one launch (start us, length us, event | category | flops | bytes accessed | tf_op | source)
XLA Modules:
  0.0 93.4 jit_solution(17735781101006802947)
XLA Ops:
  0.6 2.2 %shard_map.101 = f32[1296,128]{1,0:T(8,128)} custom-call(bf16[8,16,512]{2,1,0:T(8,128)(2,1)} %x0.1, bf16[8,16,512]{2,1,0:T(8,128)(2,1)} %y0.1, f32[8,16,16]{2,1,0:T(8,128)} %b0.1, f32[8,16,16]{2,1,0:T(8,128)} %s0.1, f32[8,8,16]{2,1,0:T(8,128)} %bitcast.24, f32[8,8,16]{2,1,0:T(8,128)} %bitcast.25), custom_call_target="tpu_custom_call" | custom-call | flops 100000000 | bytes 1000000 | tf_op jit(solution)/shard_map/pallas_call | solution.py:568
  2.8 28.3 %all_to_all.20 = f32[1296,1,128]{2,1,0:T(1,128)S(1)} all-to-all(f32[1296,1,128]{2,1,0:T(1,128)} %bitcast.23), channel_id=1, replica_groups=mesh['ha'=8,'wa'=32] {'ha'}, dimensions={0} | all-to-all | bytes 1327104 | tf_op jit(solution)/shard_map/all_to_all | solution.py:559
  31.1 2.6 %shard_map.102 = (f32[1056,128]{1,0:T(8,128)S(1)}, f32[16,64,128]{2,1,0:T(8,128)S(1)}, f32[16,40,128]{2,1,0:T(8,128)S(1)}, bf16[8,128,256]{2,1,0:T(8,128)(2,1)S(1)}) custom-call(f32[1296,128]{1,0:T(8,128)S(1)} %bitcast.16), custom_call_target="tpu_custom_call" | custom-call | flops 100000000 | bytes 1000000 | tf_op jit(solution)/shard_map/pallas_call | solution.py:572
  33.8 20.8 %all_to_all.21 = f32[1056,1,128]{2,1,0:T(1,128)S(1)} all-to-all(f32[1056,1,128]{2,1,0:T(1,128)S(1)} %bitcast.22), channel_id=1, replica_groups=mesh['ha'=8,'wa'=32] {'wa'}, dimensions={0} | all-to-all | bytes 1081344 | tf_op jit(solution)/shard_map/all_to_all | solution.py:559
  54.6 0.9 shard_map.103
  55.5 3.7 %all-to-all-start.2 = ((f32[32,32,128]{2,1,0:T(8,128)}), f32[32,32,128]{2,1,0:T(8,128)S(1)}, u32[]{:S(2)}, u32[]{:S(2)}) async-start(f32[32,32,128]{2,1,0:T(8,128)} %shard_map.103), calls=%async_computation.2 | async-start | bytes 1048576 | tf_op jit(solution)/shard_map/all_to_all | solution.py:575
  59.1 8.2 %shard_map.104 = (f32[784,128]{1,0:T(8,128)S(1)}, bf16[8,128,128]{2,1,0:T(8,128)(2,1)S(1)}, bf16[8,128,128]{2,1,0:T(8,128)(2,1)S(1)}, bf16[16,8,64,128]{3,2,1,0:T(8,128)(2,1)}, f32[16,8,64,128]{3,2,1,0:T(8,128)}) custom-call(f32[1296,128]{1,0:T(8,128)S(1)} %bitcast.17, f32[16,64,128]{2,1,0:T(8,128)S(1)} %get-tuple-element.20.back, ...), custom_call_target="tpu_custom_call" | custom-call | flops 5000000000 | bytes 1000000 | tf_op jit(solution)/shard_map/pallas_call | solution.py:574
  67.3 3.4 %all-to-all-done.2.edge = f32[32,32,128]{2,1,0:T(8,128)S(1)} async-done(((f32[32,32,128]{2,1,0:T(8,128)}), f32[32,32,128]{2,1,0:T(8,128)S(1)}, u32[]{:S(2)}, u32[]{:S(2)}) %all-to-all-start.2) | async-done | bytes 524320 | tf_op jit(solution)/shard_map/all_to_all | solution.py:575
  70.7 4.0 %shard_map.105 = f32[784,128]{1,0:T(8,128)S(1)} custom-call(f32[1296,128]{1,0:T(8,128)S(1)} %bitcast.18, f32[32,32,128]{2,1,0:T(8,128)S(1)} %all-to-all-done.2.edge, f32[784,128]{1,0:T(8,128)S(1)} %get-tuple-element.23.local, f32[16,40,128]{2,1,0:T(8,128)S(1)} %get-tuple-element.22.table, bf16[8,128,128]{2,1,0:T(8,128)(2,1)S(1)} %get-tuple-element.24.high, ...), custom_call_target="tpu_custom_call" | custom-call | flops 100000000 | bytes 1000000 | tf_op jit(solution)/shard_map/pallas_call | solution.py:576
  74.7 17.8 %all_to_all.22 = f32[784,1,128]{2,1,0:T(1,128)S(1)} all-to-all(f32[784,1,128]{2,1,0:T(1,128)S(1)} %bitcast.21), channel_id=1, replica_groups=mesh['ha'=8,'wa'=32] {'ha'}, dimensions={0} | all-to-all | bytes 802816 | tf_op jit(solution)/shard_map/all_to_all | solution.py:559
  92.5 0.9 shard_map.106
Async XLA Ops:
  55.5 15.3 %all-to-all-start.2 = ((f32[32,32,128]{2,1,0:T(8,128)}), f32[32,32,128]{2,1,0:T(8,128)S(1)}, u32[]{:S(2)}, u32[]{:S(2)}) async-start(f32[32,32,128]{2,1,0:T(8,128)} %shard_map.103), calls=%async_computation.2 | async-start | bytes 1048576 | tf_op jit(solution)/shard_map/all_to_all | solution.py:575

commit v6 on v4

--- a/solution.py
+++ b/solution.py
@@ -169,8 +169,8 @@
     move = mover(down)
     keep = inside(down)
 
-    for part in range(2):
-        cols = range(part * COLS // 2, (part + 1) * COLS // 2)
+    for part in range(1):
+        cols = range(COLS)
         values = [jnp.where(keep, move(ends[col], 1), 0.0) for col in cols]
         for k, by in enumerate((1, 2, 4)):
             moved = [move(f, by) for f in values]

time: 93.9 us -> 93.9 us (level)
  no operation moved by 1% of the time
where the time goes in v6:
time: 93.9 us; the launch traced here: 93.6 us
  blocking collectives  66.9 us (71%)
  Pallas kernels  18.9 us (20%)
  starting transfers between devices  3.68 us (4%)
  waiting for transfers between devices  3.39 us (4%)
    all_to_all x3, blocking collectives, exchange(): lax.all_to_all(a.reshape(-1, 1, LANES), axis, 0, 0, tiled=True)  66.9 us
    pallas_call x1, Pallas kernels, per_device(): local, high, low, *far = local_grads()(tile, back, place, table)  8.18 us
    pallas_call x1, Pallas kernels, per_device(): answer = outer_grads()(tile, carries, local, table, high, low, *far)  4.01 us
    all_to_all x1, starting transfers between devices, per_device(): carries = lax.all_to_all(chains(devices)(edge), 'wa', 0, 0, tiled=True)  3.68 us
    all_to_all x1, waiting for transfers between devices, per_device(): carries = lax.all_to_all(chains(devices)(edge), 'wa', 0, 0, tiled=True)  3.39 us
    pallas_call x1, Pallas kernels, per_device(): edge, back, table, place = edges(devices)(tile)  2.75 us
    pallas_call x1, Pallas kernels, per_device(): packs()  2.17 us
  transfers between devices with their start and end apart: 1, of which 1 were waited for; matrix products, arithmetic and copies ran while one was open for 0% of the time, Pallas kernels for 9%

profile of v6, /device:TPU:1, one launch (start us, length us, event | category | flops | bytes accessed | tf_op | source)
XLA Modules:
  0.0 93.6 jit_solution(2027679880695348978)
XLA Ops:
  0.6 2.2 %shard_map.101 = f32[1296,128]{1,0:T(8,128)} custom-call(bf16[8,16,512]{2,1,0:T(8,128)(2,1)} %x0.1, bf16[8,16,512]{2,1,0:T(8,128)(2,1)} %y0.1, f32[8,16,16]{2,1,0:T(8,128)} %b0.1, f32[8,16,16]{2,1,0:T(8,128)} %s0.1, f32[8,8,16]{2,1,0:T(8,128)} %bitcast.24, f32[8,8,16]{2,1,0:T(8,128)} %bitcast.25), custom_call_target="tpu_custom_call" | custom-call | flops 100000000 | bytes 1000000 | tf_op jit(solution)/shard_map/pallas_call | solution.py:562
  2.8 28.3 %all_to_all.20 = f32[1296,1,128]{2,1,0:T(1,128)S(1)} all-to-all(f32[1296,1,128]{2,1,0:T(1,128)} %bitcast.23), channel_id=1, replica_groups=mesh['ha'=8,'wa'=32] {'ha'}, dimensions={0} | all-to-all | bytes 1327104 | tf_op jit(solution)/shard_map/all_to_all | solution.py:553
  31.1 2.7 %shard_map.102 = (f32[1056,128]{1,0:T(8,128)S(1)}, f32[16,64,128]{2,1,0:T(8,128)S(1)}, f32[16,40,128]{2,1,0:T(8,128)S(1)}, bf16[8,128,256]{2,1,0:T(8,128)(2,1)S(1)}) custom-call(f32[1296,128]{1,0:T(8,128)S(1)} %bitcast.16), custom_call_target="tpu_custom_call" | custom-call | flops 100000000 | bytes 1000000 | tf_op jit(solution)/shard_map/pallas_call | solution.py:566
  33.9 20.8 %all_to_all.21 = f32[1056,1,128]{2,1,0:T(1,128)S(1)} all-to-all(f32[1056,1,128]{2,1,0:T(1,128)S(1)} %bitcast.22), channel_id=1, replica_groups=mesh['ha'=8,'wa'=32] {'wa'}, dimensions={0} | all-to-all | bytes 1081344 | tf_op jit(solution)/shard_map/all_to_all | solution.py:553
  54.7 0.9 shard_map.103
  55.6 3.7 %all-to-all-start.2 = ((f32[32,32,128]{2,1,0:T(8,128)}), f32[32,32,128]{2,1,0:T(8,128)S(1)}, u32[]{:S(2)}, u32[]{:S(2)}) async-start(f32[32,32,128]{2,1,0:T(8,128)} %shard_map.103), calls=%async_computation.2 | async-start | bytes 1048576 | tf_op jit(solution)/shard_map/all_to_all | solution.py:569
  59.3 8.2 %shard_map.104 = (f32[784,128]{1,0:T(8,128)S(1)}, bf16[8,128,128]{2,1,0:T(8,128)(2,1)S(1)}, bf16[8,128,128]{2,1,0:T(8,128)(2,1)S(1)}, bf16[16,8,64,128]{3,2,1,0:T(8,128)(2,1)}, f32[16,8,64,128]{3,2,1,0:T(8,128)}) custom-call(f32[1296,128]{1,0:T(8,128)S(1)} %bitcast.17, f32[16,64,128]{2,1,0:T(8,128)S(1)} %get-tuple-element.20.back, ...), custom_call_target="tpu_custom_call" | custom-call | flops 5000000000 | bytes 1000000 | tf_op jit(solution)/shard_map/pallas_call | solution.py:568
  67.4 3.4 %all-to-all-done.2.edge = f32[32,32,128]{2,1,0:T(8,128)S(1)} async-done(((f32[32,32,128]{2,1,0:T(8,128)}), f32[32,32,128]{2,1,0:T(8,128)S(1)}, u32[]{:S(2)}, u32[]{:S(2)}) %all-to-all-start.2) | async-done | bytes 524320 | tf_op jit(solution)/shard_map/all_to_all | solution.py:569
  70.8 4.0 %shard_map.105 = f32[784,128]{1,0:T(8,128)S(1)} custom-call(f32[1296,128]{1,0:T(8,128)S(1)} %bitcast.18, f32[32,32,128]{2,1,0:T(8,128)S(1)} %all-to-all-done.2.edge, f32[784,128]{1,0:T(8,128)S(1)} %get-tuple-element.23.local, f32[16,40,128]{2,1,0:T(8,128)S(1)} %get-tuple-element.22.table, bf16[8,128,128]{2,1,0:T(8,128)(2,1)S(1)} %get-tuple-element.24.high, ...), custom_call_target="tpu_custom_call" | custom-call | flops 100000000 | bytes 1000000 | tf_op jit(solution)/shard_map/pallas_call | solution.py:570
  74.9 17.8 %all_to_all.22 = f32[784,1,128]{2,1,0:T(1,128)S(1)} all-to-all(f32[784,1,128]{2,1,0:T(1,128)S(1)} %bitcast.21), channel_id=1, replica_groups=mesh['ha'=8,'wa'=32] {'ha'}, dimensions={0} | all-to-all | bytes 802816 | tf_op jit(solution)/shard_map/all_to_all | solution.py:553
  92.6 0.9 shard_map.106
Async XLA Ops:
  55.6 15.3 %all-to-all-start.2 = ((f32[32,32,128]{2,1,0:T(8,128)}), f32[32,32,128]{2,1,0:T(8,128)S(1)}, u32[]{:S(2)}, u32[]{:S(2)}) async-start(f32[32,32,128]{2,1,0:T(8,128)} %shard_map.103), calls=%async_computation.2 | async-start | bytes 1048576 | tf_op jit(solution)/shard_map/all_to_all | solution.py:569

commit v7 on v5

--- a/solution.py
+++ b/solution.py
@@ -169,8 +169,8 @@
     move = mover(down)
     keep = inside(down)
 
-    for part in range(2):
-        cols = range(part * COLS // 2, (part + 1) * COLS // 2)
+    for part in range(1):
+        cols = range(COLS)
         values = [jnp.where(keep, move(ends[col], 1), 0.0) for col in cols]
         for k, by in enumerate((1, 2, 4)):
             moved = [move(f, by) for f in values]

time: 93.8 us -> 93.7 us (level)
  no operation moved by 1% of the time
where the time goes in v7:
time: 93.7 us; the launch traced here: 93.4 us
  blocking collectives  66.9 us (71%)
  Pallas kernels  18.7 us (20%)
  starting transfers between devices  3.68 us (4%)
  waiting for transfers between devices  3.4 us (4%)
    all_to_all x3, blocking collectives, exchange(): lax.all_to_all(a.reshape(-1, 1, LANES), axis, 0, 0, tiled=True)  66.9 us
    pallas_call x1, Pallas kernels, per_device(): local, high, low, *far = local_grads()(tile, back, place, table)  8.18 us
    pallas_call x1, Pallas kernels, per_device(): answer = outer_grads()(tile, carries, local, table, high, low, *far)  3.98 us
    all_to_all x1, starting transfers between devices, per_device(): carries = lax.all_to_all(chains(devices)(edge), 'wa', 0, 0, tiled=True)  3.68 us
    all_to_all x1, waiting for transfers between devices, per_device(): carries = lax.all_to_all(chains(devices)(edge), 'wa', 0, 0, tiled=True)  3.4 us
    pallas_call x1, Pallas kernels, per_device(): edge, back, table, place = edges(devices)(tile)  2.62 us
    pallas_call x1, Pallas kernels, per_device(): packs()  2.17 us
  transfers between devices with their start and end apart: 1, of which 1 were waited for; matrix products, arithmetic and copies ran while one was open for 0% of the time, Pallas kernels for 9%

profile of v7, /device:TPU:1, one launch (start us, length us, event | category | flops | bytes accessed | tf_op | source)
XLA Modules:
  0.0 93.4 jit_solution(3740906655754943338)
XLA Ops:
  0.6 2.2 %shard_map.101 = f32[1296,128]{1,0:T(8,128)} custom-call(bf16[8,16,512]{2,1,0:T(8,128)(2,1)} %x0.1, bf16[8,16,512]{2,1,0:T(8,128)(2,1)} %y0.1, f32[8,16,16]{2,1,0:T(8,128)} %b0.1, f32[8,16,16]{2,1,0:T(8,128)} %s0.1, f32[8,8,16]{2,1,0:T(8,128)} %bitcast.24, f32[8,8,16]{2,1,0:T(8,128)} %bitcast.25), custom_call_target="tpu_custom_call" | custom-call | flops 100000000 | bytes 1000000 | tf_op jit(solution)/shard_map/pallas_call | solution.py:568
  2.8 28.3 %all_to_all.20 = f32[1296,1,128]{2,1,0:T(1,128)S(1)} all-to-all(f32[1296,1,128]{2,1,0:T(1,128)} %bitcast.23), channel_id=1, replica_groups=mesh['ha'=8,'wa'=32] {'ha'}, dimensions={0} | all-to-all | bytes 1327104 | tf_op jit(solution)/shard_map/all_to_all | solution.py:559
  31.1 2.6 %shard_map.102 = (f32[1056,128]{1,0:T(8,128)S(1)}, f32[16,64,128]{2,1,0:T(8,128)S(1)}, f32[16,40,128]{2,1,0:T(8,128)S(1)}, bf16[8,128,256]{2,1,0:T(8,128)(2,1)S(1)}) custom-call(f32[1296,128]{1,0:T(8,128)S(1)} %bitcast.16), custom_call_target="tpu_custom_call" | custom-call | flops 100000000 | bytes 1000000 | tf_op jit(solution)/shard_map/pallas_call | solution.py:572
  33.8 20.8 %all_to_all.21 = f32[1056,1,128]{2,1,0:T(1,128)S(1)} all-to-all(f32[1056,1,128]{2,1,0:T(1,128)S(1)} %bitcast.22), channel_id=1, replica_groups=mesh['ha'=8,'wa'=32] {'wa'}, dimensions={0} | all-to-all | bytes 1081344 | tf_op jit(solution)/shard_map/all_to_all | solution.py:559
  54.6 0.9 shard_map.103
  55.4 3.7 %all-to-all-start.2 = ((f32[32,32,128]{2,1,0:T(8,128)}), f32[32,32,128]{2,1,0:T(8,128)S(1)}, u32[]{:S(2)}, u32[]{:S(2)}) async-start(f32[32,32,128]{2,1,0:T(8,128)} %shard_map.103), calls=%async_computation.2 | async-start | bytes 1048576 | tf_op jit(solution)/shard_map/all_to_all | solution.py:575
  59.1 8.2 %shard_map.104 = (f32[784,128]{1,0:T(8,128)S(1)}, bf16[8,128,128]{2,1,0:T(8,128)(2,1)S(1)}, bf16[8,128,128]{2,1,0:T(8,128)(2,1)S(1)}, bf16[16,8,64,128]{3,2,1,0:T(8,128)(2,1)}, f32[16,8,64,128]{3,2,1,0:T(8,128)}) custom-call(f32[1296,128]{1,0:T(8,128)S(1)} %bitcast.17, f32[16,64,128]{2,1,0:T(8,128)S(1)} %get-tuple-element.20.back, ...), custom_call_target="tpu_custom_call" | custom-call | flops 5000000000 | bytes 1000000 | tf_op jit(solution)/shard_map/pallas_call | solution.py:574
  67.3 3.4 %all-to-all-done.2.edge = f32[32,32,128]{2,1,0:T(8,128)S(1)} async-done(((f32[32,32,128]{2,1,0:T(8,128)}), f32[32,32,128]{2,1,0:T(8,128)S(1)}, u32[]{:S(2)}, u32[]{:S(2)}) %all-to-all-start.2) | async-done | bytes 524320 | tf_op jit(solution)/shard_map/all_to_all | solution.py:575
  70.7 4.0 %shard_map.105 = f32[784,128]{1,0:T(8,128)S(1)} custom-call(f32[1296,128]{1,0:T(8,128)S(1)} %bitcast.18, f32[32,32,128]{2,1,0:T(8,128)S(1)} %all-to-all-done.2.edge, f32[784,128]{1,0:T(8,128)S(1)} %get-tuple-element.23.local, f32[16,40,128]{2,1,0:T(8,128)S(1)} %get-tuple-element.22.table, bf16[8,128,128]{2,1,0:T(8,128)(2,1)S(1)} %get-tuple-element.24.high, ...), custom_call_target="tpu_custom_call" | custom-call | flops 100000000 | bytes 1000000 | tf_op jit(solution)/shard_map/pallas_call | solution.py:576
  74.7 17.8 %all_to_all.22 = f32[784,1,128]{2,1,0:T(1,128)S(1)} all-to-all(f32[784,1,128]{2,1,0:T(1,128)S(1)} %bitcast.21), channel_id=1, replica_groups=mesh['ha'=8,'wa'=32] {'ha'}, dimensions={0} | all-to-all | bytes 802816 | tf_op jit(solution)/shard_map/all_to_all | solution.py:559
  92.5 0.9 shard_map.106
Async XLA Ops:
  55.4 15.3 %all-to-all-start.2 = ((f32[32,32,128]{2,1,0:T(8,128)}), f32[32,32,128]{2,1,0:T(8,128)S(1)}, u32[]{:S(2)}, u32[]{:S(2)}) async-start(f32[32,32,128]{2,1,0:T(8,128)} %shard_map.103), calls=%async_computation.2 | async-start | bytes 1048576 | tf_op jit(solution)/shard_map/all_to_all | solution.py:575
